TPU v7x, 128 devices: a whole 4x4x4 slice. The times are simulated.
128 devices in a mesh: seq: 16 (over y, x), dp: 8 (over z, core).
Axes of the slice: x: 4, y: 4, z: 4, core: 2. Of those that a mesh axis runs over, the one named last changes fastest.
Arguments:
- queries: bfloat16 [8, 2048, 4096], P('dp', 'seq'), may hold values from -6 to 12
- image_keys: bfloat16 [8, 16, 1601, 512], P('dp', 'seq'), may hold values from -6 to 12
- image_values: bfloat16 [8, 16, 1601, 512], P('dp', 'seq'), may hold values from -6 to 6
- cotangent: bfloat16 [8, 2048, 4096], P('dp', 'seq'), may hold values from -6 to 6
- gate: float32 [], replicated, may hold values from 0.3 to 1.2
- tile_list: int32 [8, 16, 2], P('dp'), may hold values from 0 to 15, as said below
- slot_range: int32 [8, 2048, 2], P('dp'), may hold values from 0 to 2, as said below
Outputs:
- attended: bfloat16 [8, 2048, 4096], P('dp', 'seq')
- query_grad: bfloat16 [8, 2048, 4096], P('dp', 'seq')
- key_grad: bfloat16 [8, 16, 1601, 512], P('dp', 'seq')
- value_grad: bfloat16 [8, 16, 1601, 512], P('dp', 'seq')
- gate_grad: float32 [], replicated
Inputs may be any that keep to these rules, and one draw needn't show every extreme that they name: `tile_list`: each row lists 2 different tiles of its batch. Tile g of a batch is held by the device at index g // 1 of seq, and block b stands on the device at index b of seq. A block's first listed tile is held by its own device, its second by a device whose index differs from its own by one. At most 3 blocks of one batch list the same tile, and in every batch some tile is listed by exactly 3 blocks. `slot_range`: for every token the first value is at most the second. A range may be empty, and a listed slot may be attended by no token of its block.
All inputs are finite; a program needn't handle non-finite values.
Results may differ from a plain program's by a relative error of at most 0.0075.
The roundings to bfloat16 on the way count: a program that leaves them out, or rounds other values in their place, can miss the bound.
Values may be sent and summed in bfloat16 or wider, within the bound.
A program may use at most 192 MiB of HBM per device.

v0:
```python
import jax
import jax.numpy as jnp
from jax import lax
from jax.sharding import PartitionSpec as P

HEADS = 32
KV_HEADS = 4
HEAD_DIM = 128
BLOCK = 128
MAXT = 2
MOST = 3
GROUP = 8


NEG_FILL = -1e30


def extended(shard, sides, width):
    for axis, dim in sides:
        count, length = (lax.axis_size(axis), shard.shape[dim])
        up = [(i, (i + 1) % count) for i in range(count - 1)]
        down = [(j, i) for i, j in up]
        last = lax.slice_in_dim(shard, length - width, length, axis=dim)
        first = lax.slice_in_dim(shard, 0, width, axis=dim)
        before = lax.ppermute(last, axis, up)
        after = lax.ppermute(first, axis, down)
        shard = jnp.concatenate([before, shard, after], axis=dim)
    return shard


def head_rows(block_rows, head):
    width = GROUP * HEAD_DIM
    return block_rows[:, head * width : (head + 1) * width].reshape(
        block_rows.shape[0], GROUP, HEAD_DIM
    )


def head_keys(tile_rows, head):
    return tile_rows[:, head * HEAD_DIM : (head + 1) * HEAD_DIM]


def outer_rows(values, rows, axis_index):
    low = lax.slice_in_dim(values, 0, rows, axis=axis_index)
    high = lax.slice_in_dim(values, 2 * rows, 3 * rows, axis=axis_index)
    return jnp.concatenate([low, high], axis_index)


def pair_forward(query_block, key_tile, value_tile, active):
    scale = HEAD_DIM ** (-0.5)
    active_mask = active[:, None]
    outputs, maxima, totals = ([], [], [])
    for head in range(KV_HEADS):
        scores = (
            jnp.einsum(
                "tgd,sd->tgs",
                head_rows(query_block, head),
                head_keys(key_tile, head),
                preferred_element_type=jnp.float32,
            )
            * scale
        )
        row_max = jnp.where(active_mask, jnp.max(scores, axis=-1), NEG_FILL)
        probs = jnp.where(active_mask[..., None], jnp.exp(scores - row_max[..., None]), 0.0)
        total = jnp.sum(probs, axis=-1)
        numerator = jnp.einsum(
            "tgs,sd->tgd",
            probs.astype(jnp.bfloat16),
            head_keys(value_tile, head),
            preferred_element_type=jnp.float32,
        )
        partial_out = jnp.where(
            active_mask[..., None], numerator / jnp.where(active_mask, total, 1.0)[..., None], 0.0
        )
        outputs.append(partial_out.reshape(partial_out.shape[0], GROUP * HEAD_DIM))
        maxima.append(row_max)
        totals.append(total)
    return (jnp.concatenate(outputs, 1), jnp.concatenate(maxima, 1), jnp.concatenate(totals, 1))


def pair_backward(query_block, key_tile, value_tile, active, grad_block, lse_block, delta_block):
    scale = HEAD_DIM ** (-0.5)
    active_mask = active[:, None]
    query_parts, key_parts, value_parts = ([], [], [])
    for head in range(KV_HEADS):
        columns = slice(head * GROUP, (head + 1) * GROUP)
        query_head = head_rows(query_block, head)
        grad_head = head_rows(grad_block, head)
        key_head = head_keys(key_tile, head)
        scores = (
            jnp.einsum("tgd,sd->tgs", query_head, key_head, preferred_element_type=jnp.float32)
            * scale
        )
        back_probs = jnp.where(
            active_mask[..., None], jnp.exp(scores - lse_block[:, columns][..., None]), 0.0
        )
        value_parts.append(
            jnp.einsum(
                "tgs,tgd->sd",
                back_probs.astype(jnp.bfloat16),
                grad_head,
                preferred_element_type=jnp.float32,
            )
        )
        prob_grad = jnp.einsum(
            "tgd,sd->tgs",
            grad_head,
            head_keys(value_tile, head),
            preferred_element_type=jnp.float32,
        )
        score_grad = (back_probs * (prob_grad - delta_block[:, columns][..., None])).astype(
            jnp.bfloat16
        )
        query_part = (
            jnp.einsum("tgs,sd->tgd", score_grad, key_head, preferred_element_type=jnp.float32)
            * scale
        )
        query_parts.append(query_part.reshape(query_part.shape[0], GROUP * HEAD_DIM))
        key_parts.append(
            jnp.einsum("tgs,tgd->sd", score_grad, query_head, preferred_element_type=jnp.float32)
            * scale
        )
    return (
        jnp.concatenate(query_parts, 1),
        jnp.concatenate(key_parts, 1),
        jnp.concatenate(value_parts, 1),
    )


def shards(queries, image_keys, image_values, cotangent, gate, tile_list, slot_range):
    groups = lax.axis_size("seq")
    position = lax.axis_index("seq")
    query_local = queries[0]
    local_rows = query_local.shape[0]
    query_width = query_local.shape[1]
    tile_dev = image_keys.shape[1]
    keys_local = image_keys[0]
    values_local = image_values[0]
    tile_tokens = keys_local.shape[1]
    key_width = keys_local.shape[2]
    listing = tile_list[0]
    ranges = slot_range[0]
    gate_tanh = jnp.tanh(gate)
    grad_local = (gate_tanh * cotangent[0].astype(jnp.float32)).astype(jnp.bfloat16)
    window = extended(jnp.stack([query_local, grad_local]), (("seq", 1),), local_rows)
    query_src = window[0]
    grad_src = window[1]
    frame_base = (position - 1) * local_rows
    frame_rows = 3 * local_rows
    owned = listing // tile_dev == position
    capacity = tile_dev * MOST
    picked = jnp.nonzero(owned.reshape(-1), size=capacity, fill_value=-1)[0].astype(jnp.int32)
    flat_listing = listing.reshape(-1)

    def pair_info(index):
        entry = picked[index]
        valid = entry >= 0
        flat = jnp.maximum(entry, 0)
        slot = flat % MAXT
        start = flat // MAXT * BLOCK
        frame_start = jnp.maximum(start - frame_base, 0).astype(jnp.int32)
        local_tile = jnp.clip(flat_listing[flat] - position * tile_dev, 0, tile_dev - 1)
        row_range = lax.dynamic_slice_in_dim(ranges, start, BLOCK, 0)
        active = (row_range[:, 0] <= slot) & (slot < row_range[:, 1])
        query_block = lax.dynamic_slice_in_dim(query_src, frame_start, BLOCK, 0)
        key_tile = lax.dynamic_index_in_dim(keys_local, local_tile, 0, keepdims=False)
        value_tile = lax.dynamic_index_in_dim(values_local, local_tile, 0, keepdims=False)
        return (valid, frame_start, active, query_block, key_tile, value_tile, local_tile)

    def forward_pair(index, carry):
        valid, start, active, query_block, key_tile, value_tile, local_tile = pair_info(index)

        def forward_work(state):
            partial_out, row_max, total = pair_forward(query_block, key_tile, value_tile, active)
            return (
                lax.dynamic_update_slice_in_dim(state[0], partial_out, start, 0),
                lax.dynamic_update_slice_in_dim(state[1], row_max, start, 0),
                lax.dynamic_update_slice_in_dim(state[2], total, start, 0),
            )

        return lax.cond(valid, forward_work, lambda state: state, carry)

    forward_init = (
        jnp.zeros((frame_rows, query_width), jnp.float32),
        jnp.full((frame_rows, HEADS), NEG_FILL, jnp.float32),
        jnp.zeros((frame_rows, HEADS), jnp.float32),
    )
    partial_outs, partial_maxima, partial_totals = lax.fori_loop(
        0, capacity, forward_pair, forward_init
    )
    back_outs = extended(outer_rows(partial_outs, local_rows, 0), (("seq", 0),), local_rows)
    stacked = outer_rows(jnp.stack([partial_maxima, partial_totals]), local_rows, 1)
    back_stats = extended(stacked, (("seq", 1),), local_rows)
    middle = slice(local_rows, 2 * local_rows)
    far = slice(3 * local_rows, 4 * local_rows)
    near = slice(0, local_rows)
    left_max = jnp.where(position > 0, back_stats[0, near], NEG_FILL)
    right_max = jnp.where(position < groups - 1, back_stats[0, far], NEG_FILL)
    got_outs = jnp.stack([back_outs[near], partial_outs[middle], back_outs[far]])
    got_maxima = jnp.stack([left_max, partial_maxima[middle], right_max])
    got_totals = jnp.stack([back_stats[1, near], partial_totals[middle], back_stats[1, far]])
    sources = got_outs.shape[0]
    top = jnp.max(got_maxima, axis=0)
    shares = got_totals * jnp.exp(got_maxima - top[None])
    whole = jnp.sum(shares, axis=0)
    merged = jnp.sum(
        shares[..., None] * got_outs.reshape(sources, local_rows, HEADS, HEAD_DIM), axis=0
    )
    own_range = lax.dynamic_slice_in_dim(ranges, position * local_rows, local_rows, 0)
    any_active = (own_range[:, 0] < own_range[:, 1])[:, None]
    combined = jnp.where(
        any_active[..., None], merged / jnp.where(any_active, whole, 1.0)[..., None], 0.0
    )
    lse = jnp.where(any_active, top + jnp.log(jnp.where(any_active, whole, 1.0)), 0.0)
    combined_flat = combined.reshape(local_rows, query_width)
    attended = (gate_tanh * combined_flat).astype(jnp.bfloat16)
    delta = jnp.sum(
        grad_local.astype(jnp.float32).reshape(local_rows, HEADS, HEAD_DIM) * combined, axis=-1
    )
    stat_frame = extended(jnp.stack([lse, delta]), (("seq", 1),), local_rows)
    lse_src = stat_frame[0]
    delta_src = stat_frame[1]

    def backward_pair(index, carry):
        valid, start, active, query_block, key_tile, value_tile, local_tile = pair_info(index)

        def backward_work(state):
            query_acc, key_acc, value_acc = state
            grad_block = lax.dynamic_slice_in_dim(grad_src, start, BLOCK, 0)
            lse_block = lax.dynamic_slice_in_dim(lse_src, start, BLOCK, 0)
            delta_block = lax.dynamic_slice_in_dim(delta_src, start, BLOCK, 0)
            query_part, key_part, value_part = pair_backward(
                query_block, key_tile, value_tile, active, grad_block, lse_block, delta_block
            )
            query_acc = lax.dynamic_update_slice_in_dim(query_acc, query_part, start, 0)
            key_old = lax.dynamic_index_in_dim(key_acc, local_tile, 0, keepdims=False)
            key_acc = lax.dynamic_update_index_in_dim(key_acc, key_old + key_part, local_tile, 0)
            value_old = lax.dynamic_index_in_dim(value_acc, local_tile, 0, keepdims=False)
            value_acc = lax.dynamic_update_index_in_dim(
                value_acc, value_old + value_part, local_tile, 0
            )
            return (query_acc, key_acc, value_acc)

        return lax.cond(valid, backward_work, lambda state: state, carry)

    backward_init = (
        jnp.zeros((frame_rows, query_width), jnp.float32),
        jnp.zeros((tile_dev, tile_tokens, key_width), jnp.float32),
        jnp.zeros((tile_dev, tile_tokens, key_width), jnp.float32),
    )
    query_terms, key_acc, value_acc = lax.fori_loop(0, capacity, backward_pair, backward_init)
    rounded = query_terms.astype(jnp.bfloat16)
    back_terms = extended(outer_rows(rounded, local_rows, 0), (("seq", 0),), local_rows)
    query_grad = (
        rounded[local_rows : 2 * local_rows].astype(jnp.float32)
        + back_terms[:local_rows].astype(jnp.float32)
        + back_terms[3 * local_rows :].astype(jnp.float32)
    )
    gate_local = jnp.sum(cotangent[0].astype(jnp.float32) * combined_flat)
    gate_grad = (1.0 - gate_tanh * gate_tanh) * lax.psum(gate_local, ("seq", "dp"))
    return (
        attended[None],
        query_grad.astype(jnp.bfloat16)[None],
        key_acc.astype(jnp.bfloat16)[None],
        value_acc.astype(jnp.bfloat16)[None],
        gate_grad,
    )


def solution(mesh):
    in_specs = (
        P("dp", "seq", None),
        P("dp", "seq", None, None),
        P("dp", "seq", None, None),
        P("dp", "seq", None),
        P(),
        P("dp", None, None),
        P("dp", None, None),
    )
    out_specs = (
        P("dp", "seq", None),
        P("dp", "seq", None),
        P("dp", "seq", None, None),
        P("dp", "seq", None, None),
        P(),
    )
    return jax.shard_map(shards, mesh=mesh, in_specs=in_specs, out_specs=out_specs, check_vma=False)
```

profile of v0, /device:TPU:0, one launch (start us, length us, event | category | flops | bytes accessed | tf_op | source)
XLA Modules:
  0.0 548.8 jit_solution(9702259723443624500)
XLA Ops:
  2.8 2.9 pad_maximum_fusion.5
  6.9 5.9 %collective-permute-start = (bf16[2,128,4096]{2,1,0:T(8,128)(2,1)}, bf16[2,128,4096]{2,1,0:T(8,128)(2,1)}, u32[]{:S(2)}, u32[]{:S(2)}) collective-permute-start(bf16[2,128,4096]{2,1,0:T(8,128)(2,1)} %pad_maximum_fusion.5), channel_id=1, source_target_pairs={{0,8},{8,16},{16,24},{24,32},{32,40},{40,48},{48,56},{56,64},{64,7... | collective-permute-start | bytes 6291464 | tf_op jit(solution)/shard_map/ppermute | solution.py:25
  17.0 38.1 %collective-permute-done.1 = bf16[2,128,4096]{2,1,0:T(8,128)(2,1)} collective-permute-done((bf16[2,128,4096]{2,1,0:T(8,128)(2,1)}, bf16[2,128,4096]{2,1,0:T(8,128)(2,1)}, u32[]{:S(2)}, u32[]{:S(2)}) %collective-permute-start.1) | collective-permute-done | bytes 2097184 | tf_op jit(solution)/shard_map/ppermute | solution.py:26
  56.2 3.5 pad_maximum_fusion.4
  62.0 2.9 copy.103
  64.9 3.1 broadcast.388
  67.9 42.2 %while.38 = (s32[]{:T(128)}, f32[384,4096]{0,1:T(8,128)}, f32[384,32]{0,1:T(8,128)S(1)}, f32[384,32]{0,1:T(8,128)S(1)}, s32[3]{0:T(128)S(1)}, /*index=5*/s32[204...) while((s32[]{:T(128)}, f32[384,4096]{0,1:T(8,128)}, ...), condition=%wide.region_15.16_spmd, body=%wide.region_4.15_spmd.sunk | while | flops 3425763840 | bytes 96018464 | solution.py:187
  69.3 37.9 %conditional.4 = ((f32[384,4096]{0,1:T(8,128)}, f32[384,32]{0,1:T(8,128)S(1)}, f32[384,32]{0,1:T(8,128)S(1)})) conditional(s32[]{:T(128)} %bitcast.229, (f32[384,4096]{0,1:T(8,128)}, f32[384,32]{0,1:T(8,128)S(1)}, f32[384,32]{0,1:T(8,128)S(1)}) %tuple.216, (s32[1]{0:T(128)}, s32[2048,2]{0,1:T(2,128)}, s32[]{:T(128)}, bf16[384,4096]{0,1:T(8,128)(2,1)}, ...), branch_computations={%region_5.5_spmd, %region_6.14_spmd} | conditional | flops 3425763840 | bytes 96018208 | solution.py:180
  80.9 5.4 fusion
  86.4 2.3 fusion.29
  96.6 10.6 %dynamic_update_slice.32 = f32[384,4096]{0,1:T(8,128)} dynamic-update-slice(f32[384,4096]{0,1:T(8,128)} %get-tuple-element.1147, f32[128,4096]{0,1:T(8,128)S(1)} %pad_maximum_fusion, s32[]{:T(128)S(6)} %max.58, s32[]{:T(128)} %constant.364.clone) | dynamic-update-slice | bytes 4194308 | tf_op jit(solution)/shard_map/while/body/eval_jaxpr/cond/branch_1_fun/dynamic_update_slice | solution.py:175
  110.2 5.6 %fusion.121 = (f32[128,4096]{0,1:T(8,128)}, f32[128,4096]{0,1:T(8,128)}, f32[128,4096]{0,1:T(8,128)}) fusion(f32[384,4096]{0,1:T(8,128)} %get-tuple-element.1212), kind=kLoop, calls=%fused_computation.189 | loop fusion | bytes 12582912 | tf_op jit(solution)/shard_map/slice | solution.py:44
  115.8 80.3 %collective-permute-start.4 = (f32[128,4096]{0,1:T(8,128)}, f32[128,4096]{0,1:T(8,128)}, u32[]{:S(2)}, u32[]{:S(2)}) collective-permute-start(f32[128,4096]{0,1:T(8,128)} %get-tuple-element.1390), channel_id=1, source_target_pairs={{0,8},{8,16},{16,24},{24,32},{32,40},{40,48},{48,56},{56,64},{64,7... | collective-permute-start | bytes 6291464 | tf_op jit(solution)/shard_map/ppermute | solution.py:25
  201.3 5.2 collective-permute-start.2
  206.5 2.8 copy.109
  209.4 35.3 %collective-permute-done.3 = f32[2,128,32]{1,2,0:T(8,128)S(1)} collective-permute-done((f32[2,128,32]{1,2,0:T(8,128)S(1)}, f32[2,128,32]{1,2,0:T(8,128)S(1)}, u32[]{:S(2)}, u32[]{:S(2)}) %collective-permute-start.3) | collective-permute-done | bytes 32800 | tf_op jit(solution)/shard_map/ppermute | solution.py:26
  244.7 3.6 fusion.104
  250.4 4.5 collective-permute-start.6
  258.6 3.0 fusion.107
  262.8 67.5 %psum.7 = f32[]{:T(128)} all-reduce(f32[]{:T(128)} %fusion.107), channel_id=1, replica_groups=mesh['seq'=16,'dp'=8] {'seq','dp'}, use_global_device_ids=true, to_apply=%region_24.25 | all-reduce | flops 1 | bytes 8 | tf_op jit(solution)/shard_map/psum | solution.py:259
  333.6 61.5 %while.39 = (s32[]{:T(128)}, bf16[384,4096]{0,1:T(8,128)(2,1)}, f32[1,1601,512]{2,1,0:T(8,128)}, f32[1,1601,512]{2,1,0:T(8,128)S(1)}, s32[3]{0:T(128)S(1)}, /*in...) while((s32[]{:T(128)}, bf16[384,4096]{0,1:T(8,128)(2,1)}, ...), condition=%wide.region_22.23_spmd, body=%wide.region_19.22_spmd.sunk | while | flops 8472048128 | bytes 189190992 | solution.py:250
  335.0 57.5 %conditional.5 = ((bf16[384,4096]{0,1:T(8,128)(2,1)}, f32[1,1601,512]{2,1,0:T(8,128)}, f32[1,1601,512]{2,1,0:T(8,128)S(1)})) conditional(s32[]{:T(128)} %bitcast.230, (bf16[384,4096]{0,1:T(8,128)(2,1)}, f32[1,1601,512]{2,1,0:T(8,128)}, f32[1,1601,512]{2,1,0:T(8,128)S(1)}) %tuple.219, (s32[1]{0:T(128)}, s32[2048,2]{0,1:T(2,128)}, s32[]{:T(128)}, ...), branch_computations={%region_20.20_spmd, %region_21.21_spmd} | conditional | flops 8472048128 | bytes 189190688 | solution.py:243
  344.1 2.9 multiply_convert_fusion.1
  353.1 2.9 multiply_convert_fusion.3
  362.1 3.0 multiply_convert_fusion.2
  371.2 3.0 multiply_convert_fusion
  381.8 10.7 %dynamic_update_slice.35 = bf16[384,4096]{0,1:T(8,128)(2,1)} dynamic-update-slice(bf16[384,4096]{0,1:T(8,128)(2,1)} %get-tuple-element.1170, bf16[128,4096]{0,1:T(8,128)(2,1)} %pad_maximum_fusion.3, s32[]{:T(128)S(6)} %max.61, s32[]{:T(128)} %constant.380.clone) | dynamic-update-slice | bytes 2097156 | tf_op jit(solution)/shard_map/while/body/eval_jaxpr/cond/branch_1_fun/dynamic_update_slice | solution.py:234
  395.1 4.8 copy.110
  401.7 116.6 %collective-permute-start.8 = (bf16[128,4096]{1,0:T(8,128)(2,1)S(1)}, bf16[128,4096]{1,0:T(8,128)(2,1)S(1)}, u32[]{:S(2)}, u32[]{:S(2)}) collective-permute-start(bf16[128,4096]{1,0:T(8,128)(2,1)S(1)} %get-tuple-element.1393), channel_id=1, source_target_pairs={{0,8},{8,16},{16,24},{24,32},{32,40},{40,48},{48,56},{56,64},{64,7... | collective-permute-start | bytes 3145736 | tf_op jit(solution)/shard_map/ppermute | solution.py:25
  522.4 18.2 %collective-permute-done.8 = bf16[128,4096]{1,0:T(8,128)(2,1)S(1)} collective-permute-done((bf16[128,4096]{1,0:T(8,128)(2,1)S(1)}, bf16[128,4096]{1,0:T(8,128)(2,1)S(1)}, u32[]{:S(2)}, u32[]{:S(2)}) %collective-permute-start.8) | collective-permute-done | bytes 1048608 | tf_op jit(solution)/shard_map/ppermute | solution.py:25
  540.6 4.2 collective-permute-done.9
  544.8 2.7 fusion.108
  (117 shorter events, 87.5 us)
Async XLA Ops:
  2.7 11.7 %copy-start.8 = (s32[1,16,2]{1,2,0:T(2,128)S(1)}, s32[1,16,2]{1,2,0:T(2,128)}, u32[]{:S(2)}) copy-start(s32[1,16,2]{1,2,0:T(2,128)} %param.20) | copy-start | bytes 388
  2.8 53.5 %copy-start.7 = (bf16[1,128,4096]{2,1,0:T(8,128)(2,1)S(1)}, bf16[1,128,4096]{2,1,0:T(8,128)(2,1)}, u32[]{:S(2)}) copy-start(bf16[1,128,4096]{2,1,0:T(8,128)(2,1)} %param.15) | copy-start | bytes 3145732
  5.6 49.4 %collective-permute-start.1 = (bf16[2,128,4096]{2,1,0:T(8,128)(2,1)}, bf16[2,128,4096]{2,1,0:T(8,128)(2,1)}, u32[]{:S(2)}, u32[]{:S(2)}) collective-permute-start(bf16[2,128,4096]{2,1,0:T(8,128)(2,1)} %pad_maximum_fusion.5), channel_id=1, source_target_pairs={{8,0},{16,8},{24,16},{32,24},{40,32},{48,40},{56,48},{64,56},{72,6... | collective-permute-start | bytes 6291464 | tf_op jit(solution)/shard_map/ppermute | solution.py:26
  6.9 49.3 %collective-permute-start = (bf16[2,128,4096]{2,1,0:T(8,128)(2,1)}, bf16[2,128,4096]{2,1,0:T(8,128)(2,1)}, u32[]{:S(2)}, u32[]{:S(2)}) collective-permute-start(bf16[2,128,4096]{2,1,0:T(8,128)(2,1)} %pad_maximum_fusion.5), channel_id=1, source_target_pairs={{0,8},{8,16},{16,24},{24,32},{32,40},{40,48},{48,56},{56,64},{64,7... | collective-permute-start | bytes 6291464 | tf_op jit(solution)/shard_map/ppermute | solution.py:25
  115.8 90.7 %copy-start.3 = (bf16[384,4096]{1,0:T(8,128)(2,1)S(1)}, bf16[384,4096]{1,0:T(8,128)(2,1)}, u32[]{:S(2)}) copy-start(bf16[384,4096]{1,0:T(8,128)(2,1)} %get-tuple-element.1388) | copy-start | bytes 9437188
  115.8 128.9 %collective-permute-start.4 = (f32[128,4096]{0,1:T(8,128)}, f32[128,4096]{0,1:T(8,128)}, u32[]{:S(2)}, u32[]{:S(2)}) collective-permute-start(f32[128,4096]{0,1:T(8,128)} %get-tuple-element.1390), channel_id=1, source_target_pairs={{0,8},{8,16},{16,24},{24,32},{32,40},{40,48},{48,56},{56,64},{64,7... | collective-permute-start | bytes 6291464 | tf_op jit(solution)/shard_map/ppermute | solution.py:25
  196.1 48.6 %collective-permute-start.5 = (f32[128,4096]{0,1:T(8,128)}, f32[128,4096]{0,1:T(8,128)}, u32[]{:S(2)}, u32[]{:S(2)}) collective-permute-start(f32[128,4096]{0,1:T(8,128)} %get-tuple-element.1391), channel_id=1, source_target_pairs={{8,0},{16,8},{24,16},{32,24},{40,32},{48,40},{56,48},{64,56},{72,6... | collective-permute-start | bytes 6291464 | tf_op jit(solution)/shard_map/ppermute | solution.py:26
  200.0 44.6 %collective-permute-start.3 = (f32[2,128,32]{1,2,0:T(8,128)S(1)}, f32[2,128,32]{1,2,0:T(8,128)S(1)}, u32[]{:S(2)}, u32[]{:S(2)}) collective-permute-start(f32[2,128,32]{1,2,0:T(8,128)S(1)} %get-tuple-element.1397), channel_id=1, source_target_pairs={{8,0},{16,8},{24,16},{32,24},{40,32},{48,40},{56,48},{64,56},{72,6... | collective-permute-start | bytes 98312 | tf_op jit(solution)/shard_map/ppermute | solution.py:26
  201.3 43.3 %collective-permute-start.2 = (f32[2,128,32]{1,2,0:T(8,128)S(1)}, f32[2,128,32]{1,2,0:T(8,128)S(1)}, u32[]{:S(2)}, u32[]{:S(2)}) collective-permute-start(f32[2,128,32]{1,2,0:T(8,128)S(1)} %get-tuple-element.1398), channel_id=1, source_target_pairs={{0,8},{8,16},{16,24},{24,32},{32,40},{40,48},{48,56},{56,64},{64,7... | collective-permute-start | bytes 98312 | tf_op jit(solution)/shard_map/ppermute | solution.py:25
  244.7 3.6 copy-start.4
  249.1 81.9 %collective-permute-start.7 = (f32[2,128,32]{1,2,0:T(8,128)S(1)}, f32[2,128,32]{1,2,0:T(8,128)S(1)}, u32[]{:S(2)}, u32[]{:S(2)}) collective-permute-start(f32[2,128,32]{1,2,0:T(8,128)S(1)} %pad_maximum_fusion.9), channel_id=1, source_target_pairs={{8,0},{16,8},{24,16},{32,24},{40,32},{48,40},{56,48},{64,56},{72,6... | collective-permute-start | bytes 98312 | tf_op jit(solution)/shard_map/ppermute | solution.py:26
  250.4 80.6 %collective-permute-start.6 = (f32[2,128,32]{1,2,0:T(8,128)S(1)}, f32[2,128,32]{1,2,0:T(8,128)S(1)}, u32[]{:S(2)}, u32[]{:S(2)}) collective-permute-start(f32[2,128,32]{1,2,0:T(8,128)S(1)} %pad_maximum_fusion.9), channel_id=1, source_target_pairs={{0,8},{8,16},{16,24},{24,32},{32,40},{40,48},{48,56},{56,64},{64,7... | collective-permute-start | bytes 98312 | tf_op jit(solution)/shard_map/ppermute | solution.py:25
  254.9 3.7 copy-start.6
  258.6 3.0 copy-start.5
  375.9 2.1 copy-start
  380.1 1.7 copy-start.1
  401.6 119.4 %copy-start.2 = (f32[1,1601,512]{2,1,0:T(8,128)S(1)}, f32[1,1601,512]{2,1,0:T(8,128)}, u32[]{:S(2)}) copy-start(f32[1,1601,512]{2,1,0:T(8,128)} %get-tuple-element.1214) | copy-start | bytes 9836548
  401.7 139.0 %collective-permute-start.8 = (bf16[128,4096]{1,0:T(8,128)(2,1)S(1)}, bf16[128,4096]{1,0:T(8,128)(2,1)S(1)}, u32[]{:S(2)}, u32[]{:S(2)}) collective-permute-start(bf16[128,4096]{1,0:T(8,128)(2,1)S(1)} %get-tuple-element.1393), channel_id=1, source_target_pairs={{0,8},{8,16},{16,24},{24,32},{32,40},{40,48},{48,56},{56,64},{64,7... | collective-permute-start | bytes 3145736 | tf_op jit(solution)/shard_map/ppermute | solution.py:25
  518.3 26.5 %collective-permute-start.9 = (bf16[128,4096]{1,0:T(8,128)(2,1)S(1)}, bf16[128,4096]{1,0:T(8,128)(2,1)S(1)}, u32[]{:S(2)}, u32[]{:S(2)}) collective-permute-start(bf16[128,4096]{1,0:T(8,128)(2,1)S(1)} %get-tuple-element.1394), channel_id=1, source_target_pairs={{8,0},{16,8},{24,16},{32,24},{40,32},{48,40},{56,48},{64,56},{72,6... | collective-permute-start | bytes 3145736 | tf_op jit(solution)/shard_map/ppermute | solution.py:26
where the time goes:
time: 556 us; the launch traced here: 549 us
  starting transfers between devices  219 us (39%)
  waiting for transfers between devices  96.9 us (17%)
  blocking collectives  67.5 us (12%)
  local copies, waits for them, and re-layouts  67.1 us (12%)
  matrix products  53.5 us (10%)
  other arithmetic  34.7 us (6%)
  loops' own time  6.38 us (1%)
    ppermute x5, starting transfers between devices, extended(): before = lax.ppermute(last, axis, up)  213 us
    ppermute x5, waiting for transfers between devices, extended(): after = lax.ppermute(first, axis, down)  77.5 us
    psum x1, blocking collectives, shards(): lax.psum(gate_local, ('seq', 'dp'))  67.5 us
    ppermute x5, waiting for transfers between devices, extended(): before = lax.ppermute(last, axis, up)  19.4 us
    dot_general x4, matrix products, pair_backward(): jnp.einsum('tgd,sd->tgs', grad_head, head_keys(value_tile, head), preferr...  11.8 us
  transfers between devices with their start and end apart: 10, of which 5 were waited for; matrix products, arithmetic and copies ran while one was open for 4% of the time, Pallas kernels for 0%

commit v1 on v0

v1 whole, which is shorter than its diff:
```python
import functools

import jax
import jax.numpy as jnp
from jax import lax
from jax.experimental import pallas as pl
from jax.experimental.pallas import tpu as pltpu
from jax.sharding import PartitionSpec as P

KV = 4
GROUP = 8
HD = 128
BLK = 128
KEYS = 1601
KEYS_MAIN = 1600
KEYS_ROWS = 1616
KEYS_WIDE = 1664
WIDTH = GROUP * HD
PARTS = 4
ROWS = 2 * BLK
CUTS = ((0, 512), (512, 512), (1024, 512), (1536, 80))
UNITS = 3 * KV
LAG = 4
SLOTS = LAG + 1
LOW = -1e30
SCALE = HD**-0.5
LOG2E = 1.4426950408889634
FACTOR = SCALE * LOG2E
F32 = jnp.float32
BF16 = jnp.bfloat16
MESH = pl.DeviceIdType.MESH
NT = (((1,), (1,)), ((), ()))


def mm(a, b):
    return jnp.dot(a, b, preferred_element_type=F32)


def mm_nt(a, b):
    return lax.dot_general(a, b, NT, preferred_element_type=F32)


def stack_rows(pair):
    return jnp.concatenate([pair[:, :HD], pair[:, HD:]], axis=0)


def turn(pair):
    return jnp.concatenate([pair[:, :HD].T, pair[:, HD:].T], axis=1)


def kernel(
    ring,
    rounds,
    gate_ref,
    mask_ref,
    ktail_ref,
    vtail_ref,
    q_hbm,
    cot_hbm,
    k_hbm,
    v_hbm,
    att_hbm,
    dq_hbm,
    dk_hbm,
    dv_hbm,
    gsum_ref,
    qb,
    cb,
    kp,
    vp,
    kt,
    vt,
    ret_o,
    ret_q,
    own_o,
    onum,
    pbuf,
    dk_acc,
    dv_acc,
    stats,
    stats_out,
    stats_in,
    lse_out,
    lse_in,
    cvec,
    gacc,
    gsend,
    grecv,
    s_kv,
    s_own,
    s_q,
    s_c,
    s_stat,
    s_lse,
    s_ro,
    s_rq,
    s_out,
    s_kvout,
    s_g,
):
    me = lax.axis_index("seq")
    dpi = lax.axis_index("dp")
    right = lax.rem(me + 1, ring)
    left = lax.rem(me + ring - 1, ring)
    tanh = gate_ref[0, 0]

    def cols(h):
        return pl.ds(pl.multiple_of(h * WIDTH, WIDTH), WIDTH)

    def to_side(d):
        return right if d == 0 else left

    def send_q(d, h):
        return pltpu.make_async_remote_copy(
            src_ref=q_hbm.at[:, cols(h)],
            dst_ref=qb.at[d, h],
            send_sem=s_q.at[0, d, h],
            recv_sem=s_q.at[1, d, h],
            device_id={"seq": to_side(d)},
            device_id_type=MESH,
        )

    def send_c(d, h):
        return pltpu.make_async_remote_copy(
            src_ref=cot_hbm.at[:, cols(h)],
            dst_ref=cb.at[d, h],
            send_sem=s_c.at[0, d, h],
            recv_sem=s_c.at[1, d, h],
            device_id={"seq": to_side(d)},
            device_id_type=MESH,
        )

    def send_stat(p, h):
        return pltpu.make_async_remote_copy(
            src_ref=stats_out.at[p, h],
            dst_ref=stats_in.at[1 - p, h],
            send_sem=s_stat.at[0, p, h],
            recv_sem=s_stat.at[1, 1 - p, h],
            device_id={"seq": to_side(1 - p)},
            device_id_type=MESH,
        )

    def send_lse(d, h):
        return pltpu.make_async_remote_copy(
            src_ref=lse_out.at[h],
            dst_ref=lse_in.at[d, h],
            send_sem=s_lse.at[0, d, h],
            recv_sem=s_lse.at[1, d, h],
            device_id={"seq": to_side(d)},
            device_id_type=MESH,
        )

    def send_ro(p, h):
        return pltpu.make_async_remote_copy(
            src_ref=cb.at[p, h],
            dst_ref=ret_o.at[1 - p, h],
            send_sem=s_ro.at[0, p, h],
            recv_sem=s_ro.at[1, 1 - p, h],
            device_id={"seq": to_side(1 - p)},
            device_id_type=MESH,
        )

    def send_rq(p, h):
        return pltpu.make_async_remote_copy(
            src_ref=qb.at[p, h],
            dst_ref=ret_q.at[1 - p, h],
            send_sem=s_rq.at[0, p, h],
            recv_sem=s_rq.at[1, 1 - p, h],
            device_id={"seq": to_side(1 - p)},
            device_id_type=MESH,
        )

    def gate_partner(r):
        name, place, bit = ("seq", me, r) if r < rounds[0] else ("dp", dpi, r - rounds[0])
        stride = 1 << bit
        return {name: place + stride * (1 - 2 * ((place // stride) % 2))}

    def send_gate(r):
        return pltpu.make_async_remote_copy(
            src_ref=gsend.at[r],
            dst_ref=grecv.at[r],
            send_sem=s_g.at[0, r],
            recv_sem=s_g.at[1, r],
            device_id=gate_partner(r),
            device_id_type=MESH,
        )

    own_q = lambda h: pltpu.make_async_copy(q_hbm.at[:, cols(h)], qb.at[2, h], s_own.at[0, h])
    own_c = lambda h: pltpu.make_async_copy(cot_hbm.at[:, cols(h)], cb.at[2, h], s_own.at[1, h])

    def load_kv(which, h):
        src, dst = ((k_hbm, kp), (v_hbm, vp))[which]
        lanes = pl.ds(pl.multiple_of(h * HD, HD), HD)
        return pltpu.make_async_copy(
            src.at[pl.ds(0, KEYS_MAIN), lanes],
            dst.at[h, pl.ds(0, KEYS_MAIN)],
            s_kv.at[which, h],
        )

    def store_kv(which, h):
        src, dst = ((kp, dk_hbm), (vp, dv_hbm))[which]
        return pltpu.make_async_copy(
            src.at[h, pl.ds(0, KEYS_ROWS)], dst.at[h], s_kvout.at[which, h]
        )

    def store_att(h):
        return pltpu.make_async_copy(cb.at[2, h], att_hbm.at[:, cols(h)], s_out.at[0, h])

    def store_dq(h):
        return pltpu.make_async_copy(qb.at[2, h], dq_hbm.at[:, cols(h)], s_out.at[1, h])

    for h in range(KV):
        for which in range(2):
            load_kv(which, h).start()
    for h in range(KV):
        own_q(h).start()
        own_c(h).start()

    total_rounds = rounds[0] + rounds[1]
    barrier = pltpu.get_barrier_semaphore()
    for side in (left, right):
        pl.semaphore_signal(barrier, inc=1, device_id={"seq": side}, device_id_type=MESH)
    for r in range(total_rounds):
        pl.semaphore_signal(barrier, inc=1, device_id=gate_partner(r), device_id_type=MESH)
    pl.semaphore_wait(barrier, 2 + total_rounds)

    for h in range(KV):
        for d in range(2):
            send_q(d, h).start()
        for d in range(2):
            send_c(d, h).start()

    gacc[...] = jnp.zeros_like(gacc)

    def prepare(h, _):
        for which in range(2):
            load_kv(which, h).wait()
        lanes = pl.ds(pl.multiple_of(h * HD, HD), HD)
        for tail, dst, flipped in ((ktail_ref, kp, kt), (vtail_ref, vp, vt)):
            dst[h, KEYS_MAIN:KEYS_ROWS, :] = tail[:, lanes]
            dst[h, KEYS_ROWS:, :] = jnp.zeros((KEYS_WIDE - KEYS_ROWS, HD), BF16)
            for j in range(KEYS_WIDE // HD):
                piece = dst[h, j * HD : (j + 1) * HD, :]
                flipped[h, :, j * HD : (j + 1) * HD] = piece.T
        return 0

    lax.fori_loop(0, KV, prepare, 0)

    def combine(h):
        send_stat(0, h).wait_recv()
        send_stat(1, h).wait_recv()
        mine = stats_out[2, h]
        low = stats_in[0, h]
        high = stats_in[1, h]
        top = jnp.maximum(jnp.maximum(mine[0], low[0]), high[0])
        shares = [one[1] * jnp.exp2(one[0] - top) for one in (mine, low, high)]
        whole = shares[0] + shares[1] + shares[2]
        some = whole > 0.0
        safe = jnp.where(some, whole, 1.0)
        delta = (shares[0] * mine[2] + shares[1] * low[2] + shares[2] * high[2]) / safe
        gamma = (shares[0] * mine[3] + shares[1] * low[3] + shares[2] * high[3]) / safe
        lse_out[h, 0] = jnp.where(some, top + jnp.log(safe) * LOG2E, 0.0)
        lse_out[h, 1] = jnp.where(some, delta, 0.0)
        gacc[...] += jnp.where(some, gamma, 0.0)
        for d in range(2):
            send_lse(d, h).start()

    def finalize(h):
        for p in range(2):
            send_ro(p, h).wait_recv()
            send_rq(p, h).wait_recv()
        cb[2, h] = (own_o[h] + ret_o[0, h].astype(F32) + ret_o[1, h].astype(F32)).astype(BF16)
        qb[2, h] = (
            qb[2, h].astype(F32) + ret_q[0, h].astype(F32) + ret_q[1, h].astype(F32)
        ).astype(BF16)
        store_att(h).start()
        store_dq(h).start()

    def forward_chunk(u, c):
        h, p, slot = u // 3, u % 3, u % SLOTS
        lanes = pl.ds(pl.multiple_of(c * ROWS, ROWS), ROWS)
        query = stack_rows(qb[p, h, :, lanes])
        row_max = None
        for start, size in CUTS:
            scores = mm_nt(kp[h, start : start + size, :], query)
            if start + size > KEYS:
                position = lax.broadcasted_iota(jnp.int32, scores.shape, 0)
                scores = jnp.where(position < KEYS - start, scores, LOW)
            pbuf[slot, c, start : start + size, :] = scores
            part = jnp.max(scores, axis=0, keepdims=True)
            row_max = part if row_max is None else jnp.maximum(row_max, part)
        row_max = row_max * FACTOR
        total = jnp.zeros((1, ROWS), F32)
        out = jnp.zeros((HD, ROWS), F32)
        for start, size in CUTS:
            probs = jnp.exp2(pbuf[slot, c, start : start + size, :] * FACTOR - row_max)
            pbuf[slot, c, start : start + size, :] = probs
            total = total + jnp.sum(probs, axis=0, keepdims=True)
            out = out + mm(vt[h, :, start : start + size], probs.astype(BF16))
        onum[slot, c] = out
        cot = turn(cb[p, h, :, lanes].astype(F32))
        grad = (tanh * cot).astype(BF16).astype(F32)
        delta = jnp.sum(grad * out, axis=0, keepdims=True) / total
        gamma = jnp.sum(cot * out, axis=0, keepdims=True) / total
        for kind, row in enumerate((row_max, total, delta, gamma)):
            for g in range(2):
                stats[slot, kind, pl.ds(2 * c + g, 1), :] = row[:, g * BLK : (g + 1) * BLK]

    def backward_chunk(u, c):
        h, p, slot = u // 3, u % 3, u % SLOTS
        lanes = pl.ds(pl.multiple_of(c * ROWS, ROWS), ROWS)
        query = stack_rows(qb[p, h, :, lanes])
        grad = (tanh * stack_rows(cb[p, h, :, lanes]).astype(F32)).astype(BF16)
        rows = [cvec[i, pl.ds(2 * c + g, 1), :] for i in range(2) for g in range(2)]
        weight = jnp.concatenate(rows[:2], axis=1)
        delta = jnp.concatenate(rows[2:], axis=1)
        turned = jnp.zeros((HD, ROWS), F32)
        for start, size in CUTS:
            keys = slice(start, start + size)
            probs = pbuf[slot, c, keys, :] * weight
            prob_grad = mm_nt(vp[h, keys, :], grad)
            score_grad = (probs * (prob_grad - delta)).astype(BF16)
            dv_acc[keys, :] += mm(probs.astype(BF16), grad)
            dk_acc[keys, :] += mm(score_grad, query)
            turned = turned + mm(kt[h, :, keys], score_grad)
        turned = turned * SCALE
        out = onum[slot, c] * (weight * tanh)
        dq = jnp.concatenate([turned[:, :BLK].T, turned[:, BLK:].T], axis=1).astype(BF16)
        out = jnp.concatenate([out[:, :BLK].T, out[:, BLK:].T], axis=1)
        qb[p, h, :, lanes] = dq

        @pl.when(p < 2)
        def _():
            cb[p, h, :, lanes] = out.astype(BF16)

        @pl.when(p == 2)
        def _():
            own_o[h, :, lanes] = out

    def forward_start(u):
        h, p = u // 3, u % 3

        for d in range(2):

            @pl.when(p == d)
            def _():
                send_q(d, h).wait_recv()
                send_c(d, h).wait_recv()

        @pl.when(p == 2)
        def _():
            own_q(h).wait()
            own_c(h).wait()

    def forward_end(u):
        h, p, slot = u // 3, u % 3, u % SLOTS
        on = mask_ref[p] > 0.0
        for kind, fill in enumerate((LOW, 0.0, 0.0, 0.0)):
            stats_out[p, h, kind] = jnp.where(on, stats[slot, kind], fill)
        for d in range(2):

            @pl.when(p == d)
            def _():
                send_stat(d, h).start()

    def backward_start(u):
        h, p, slot = u // 3, u % 3, u % SLOTS
        on = mask_ref[p] > 0.0
        for d in range(2):

            @pl.when(p == d)
            def _():
                send_lse(d, h).wait_recv()
                cvec[0] = jnp.where(on, jnp.exp2(stats[slot, 0] - lse_in[d, h, 0]), 0.0)
                cvec[1] = lse_in[d, h, 1]

        @pl.when(p == 2)
        def _():
            cvec[0] = jnp.where(on, jnp.exp2(stats[slot, 0] - lse_out[h, 0]), 0.0)
            cvec[1] = lse_out[h, 1]

        @pl.when(p == 0)
        def _():
            dk_acc[...] = jnp.zeros_like(dk_acc)
            dv_acc[...] = jnp.zeros_like(dv_acc)

    def backward_end(u):
        h, p = u // 3, u % 3
        for d in range(2):

            @pl.when(p == d)
            def _():
                send_ro(d, h).start()
                send_rq(d, h).start()

        @pl.when(p == 2)
        def _():
            kp[h, :KEYS_ROWS, :] = (dk_acc[...] * SCALE).astype(BF16)
            vp[h, :KEYS_ROWS, :] = dv_acc[...].astype(BF16)
            for which in range(2):
                store_kv(which, h).start()

    def events(u):
        @pl.when((u >= 3) & (u <= UNITS) & (u % 3 == 0))
        def _():
            combine(u // 3 - 1)

        @pl.when((u >= LAG + 3) & ((u - LAG) % 3 == 0))
        def _():
            finalize((u - LAG) // 3 - 1)

    def head_step(u, _):
        forward_start(u)
        events(u)
        lax.fori_loop(0, PARTS, lambda c, x: (forward_chunk(u, c), x)[1], 0)
        forward_end(u)
        return 0

    def main_step(u, _):
        forward_start(u)
        events(u)
        backward_start(u - LAG)

        def both(c, x):
            forward_chunk(u, c)
            backward_chunk(u - LAG, c)
            return x

        lax.fori_loop(0, PARTS, both, 0)
        forward_end(u)
        backward_end(u - LAG)
        return 0

    def gate_round(r):
        if r > 0:
            send_gate(r - 1).wait_recv()
            gacc[...] += grecv[r - 1]
        if r < total_rounds:
            gsend[r] = gacc[...]
            send_gate(r).start()

    def tail_step(u, _):
        events(u)
        backward_start(u - LAG)

        def one(c, x):
            backward_chunk(u - LAG, c)
            place = (u - UNITS) * PARTS + c
            for r in range(total_rounds + 1):

                @pl.when(place == 2 * r)
                def _():
                    gate_round(r)

            return x

        lax.fori_loop(0, PARTS, one, 0)
        backward_end(u - LAG)
        return 0

    lax.fori_loop(0, LAG, head_step, 0)
    lax.fori_loop(LAG, UNITS, main_step, 0)
    lax.fori_loop(UNITS, UNITS + LAG, tail_step, 0)
    finalize(KV - 1)
    gsum_ref[...] = gacc[...]

    for r in range(total_rounds):
        send_gate(r).wait_send()
    for h in range(KV):
        for d in range(2):
            send_q(d, h).wait_send()
            send_c(d, h).wait_send()
            send_stat(d, h).wait_send()
            send_lse(d, h).wait_send()
            send_ro(d, h).wait_send()
            send_rq(d, h).wait_send()
            store_kv(d, h).wait()
        store_att(h).wait()
        store_dq(h).wait()


def tail_rows(tile):
    return jnp.pad(tile[KEYS_MAIN:], ((0, KEYS_ROWS - KEYS), (0, 0)))


def shards(ring, rounds, queries, image_keys, image_values, cotangent, gate, tile_list, slot_range):
    position = lax.axis_index("seq")
    keys, values = image_keys[0, 0], image_values[0, 0]
    tanh = jnp.tanh(gate)
    blocks = tile_list.shape[1]
    ranges = slot_range[0].reshape(blocks, BLK, 2)
    block = jnp.arange(blocks)[None, :]
    side = position + jnp.array([-1, 1, 0])[:, None]
    slot = jnp.array([1, 1, 0])[:, None]
    listed = jnp.where(slot == 1, tile_list[0, :, 1][None], tile_list[0, :, 0][None])
    chosen = (block == side) & (listed == position)
    active = (ranges[None, :, :, 0] <= slot[..., None]) & (slot[..., None] < ranges[None, :, :, 1])
    masks = jnp.any(chosen[..., None] & active, axis=1).astype(F32).reshape(3, 1, BLK)

    any_spec = pl.BlockSpec(memory_space=pl.ANY)
    vmem_spec = pl.BlockSpec(memory_space=pltpu.VMEM)
    sems = lambda *shape: pltpu.SemaphoreType.DMA(shape)
    total_rounds = rounds[0] + rounds[1]
    attended, query_grad, key_out, value_out, gate_sum = pl.pallas_call(
        functools.partial(kernel, ring, rounds),
        out_shape=(
            jax.ShapeDtypeStruct((BLK, KV * WIDTH), BF16),
            jax.ShapeDtypeStruct((BLK, KV * WIDTH), BF16),
            jax.ShapeDtypeStruct((KV, KEYS_ROWS, HD), BF16),
            jax.ShapeDtypeStruct((KV, KEYS_ROWS, HD), BF16),
            jax.ShapeDtypeStruct((GROUP, BLK), F32),
        ),
        in_specs=[pl.BlockSpec(memory_space=pltpu.SMEM)] + [vmem_spec] * 3 + [any_spec] * 4,
        out_specs=(any_spec,) * 4 + (vmem_spec,),
        scratch_shapes=[
            pltpu.VMEM((3, KV, BLK, WIDTH), BF16),
            pltpu.VMEM((3, KV, BLK, WIDTH), BF16),
            pltpu.VMEM((KV, KEYS_WIDE, HD), BF16),
            pltpu.VMEM((KV, KEYS_WIDE, HD), BF16),
            pltpu.VMEM((KV, HD, KEYS_WIDE), BF16),
            pltpu.VMEM((KV, HD, KEYS_WIDE), BF16),
            pltpu.VMEM((2, KV, BLK, WIDTH), BF16),
            pltpu.VMEM((2, KV, BLK, WIDTH), BF16),
            pltpu.VMEM((KV, BLK, WIDTH), F32),
            pltpu.VMEM((SLOTS, PARTS, HD, ROWS), F32),
            pltpu.VMEM((SLOTS, PARTS, KEYS_ROWS, ROWS), F32),
            pltpu.VMEM((KEYS_ROWS, HD), F32),
            pltpu.VMEM((KEYS_ROWS, HD), F32),
            pltpu.VMEM((SLOTS, 4, GROUP, BLK), F32),
            pltpu.VMEM((3, KV, 4, GROUP, BLK), F32),
            pltpu.VMEM((2, KV, 4, GROUP, BLK), F32),
            pltpu.VMEM((KV, 2, GROUP, BLK), F32),
            pltpu.VMEM((2, KV, 2, GROUP, BLK), F32),
            pltpu.VMEM((2, GROUP, BLK), F32),
            pltpu.VMEM((GROUP, BLK), F32),
            pltpu.VMEM((total_rounds, GROUP, BLK), F32),
            pltpu.VMEM((total_rounds, GROUP, BLK), F32),
            sems(2, KV),
            sems(2, KV),
            sems(2, 2, KV),
            sems(2, 2, KV),
            sems(2, 2, KV),
            sems(2, 2, KV),
            sems(2, 2, KV),
            sems(2, 2, KV),
            sems(2, KV),
            sems(2, KV),
            sems(2, total_rounds),
        ],
        compiler_params=pltpu.CompilerParams(
            collective_id=0, has_side_effects=True, vmem_limit_bytes=64 * 1024 * 1024 - 65536
        ),
        cost_estimate=pl.CostEstimate(
            flops=2 * 6 * UNITS * 1024 * KEYS * HD,
            bytes_accessed=11_000_000,
            transcendentals=UNITS * 1024 * KEYS,
        ),
    )(
        tanh.reshape(1, 1),
        masks,
        tail_rows(keys),
        tail_rows(values),
        queries[0],
        cotangent[0],
        keys,
        values,
    )

    def tile_of(grad):
        return jnp.transpose(grad[:, :KEYS], (1, 0, 2)).reshape(1, 1, KEYS, KV * HD)

    gate_grad = (1.0 - tanh * tanh) * jnp.sum(gate_sum)
    return attended[None], query_grad[None], tile_of(key_out), tile_of(value_out), gate_grad


def solution(mesh):
    ring = mesh.shape["seq"]
    rounds = (ring.bit_length() - 1, mesh.shape["dp"].bit_length() - 1)
    in_specs = (
        P("dp", "seq", None),
        P("dp", "seq", None, None),
        P("dp", "seq", None, None),
        P("dp", "seq", None),
        P(),
        P("dp", None, None),
        P("dp", None, None),
    )
    out_specs = (
        P("dp", "seq", None),
        P("dp", "seq", None),
        P("dp", "seq", None, None),
        P("dp", "seq", None, None),
        P(),
    )
    return jax.shard_map(
        functools.partial(shards, ring, rounds),
        mesh=mesh,
        in_specs=in_specs,
        out_specs=out_specs,
        check_vma=False,
    )
```

time: 556 us -> 203 us (0.37); the launches traced: 549 us -> 202 us
  starting transfers between devices: 219 us -> 0 us
  Pallas kernels: 0 us -> 177 us
  waiting for transfers between devices: 96.9 us -> 0 us
  blocking collectives: 67.5 us -> 0 us
  matrix products: 53.5 us -> 0 us
  local copies, waits for them, and re-layouts: 67.1 us -> 19.2 us
  other arithmetic: 34.7 us -> 3.43 us
  loops' own time: 6.38 us -> 0 us
    ppermute x10 -> x0, starting transfers between devices: 219 us -> none  [the longest x5 213 us: extended(): before = lax.ppermute(last, axis, up)]
    pallas_call x0 -> x1, Pallas kernels: none -> 177 us  [shards(): pl.pallas_call(functools.partial(kernel, ring, rounds), out_shape=(jax.Sh...]
    ppermute x10 -> x0, waiting for transfers between devices: 96.9 us -> none  [the longest x5 77.5 us: extended(): after = lax.ppermute(first, axis, down)]
    psum x1 -> x0, blocking collectives: 67.5 us -> none  [shards(): lax.psum(gate_local, ('seq', 'dp'))]
    dot_general x28 -> x0, matrix products: 53.5 us -> none  [the longest x4 11.8 us: pair_backward(): jnp.einsum('tgd,sd->tgs', grad_head, head_keys(value_tile, head), preferr...]
    dynamic_update_slice x4 -> x0, local copies, waits for them, and re-layouts: 22 us -> none  [the longest x1 10.7 us: backward_work(): query_acc = lax.dynamic_update_slice_in_dim(query_acc, query_part, start, 0)]
    slice x7 -> x2, local copies, waits for them, and re-layouts: 13.9 us -> 1.4 us  [tail_rows(): return jnp.pad(tile[KEYS_MAIN:], ((0, KEYS_ROWS - KEYS), (0, 0)))]
    reduce_sum x6 -> x1, other arithmetic: 13.2 us -> 1.28 us  [shards(): gate_grad = (1.0 - tanh * tanh) * jnp.sum(gate_sum)]
  transfers between devices with their start and end apart: 10 -> 0, of which waited for: 5 -> 0; matrix products, arithmetic and copies ran while one was open for 4% -> 0% of each run, Pallas kernels for 0% -> 0%
where the time goes in v1:
time: 203 us; the launch traced here: 202 us
  Pallas kernels  177 us (87%)
  local copies, waits for them, and re-layouts  19.2 us (9%)
  other arithmetic  3.43 us (2%)
  between operations  3.15 us (2%)
    pallas_call x1, Pallas kernels, shards(): pl.pallas_call(functools.partial(kernel, ring, rounds), out_shape=(jax.Sh...  177 us
    unnamed x9, local copies, waits for them, and re-layouts  7.81 us
    transpose x3, local copies, waits for them, and re-layouts, tile_of(): return jnp.transpose(grad[:, :KEYS], (1, 0, 2)).reshape(1, 1, KEYS, KV * HD)  7.47 us

profile of v1, /device:TPU:0, one launch (start us, length us, event | category | flops | bytes accessed | tf_op | source)
XLA Modules:
  0.0 202.5 jit_solution(11580487580191001676)
XLA Ops:
  1.3 0.7 broadcast_add_fusion
  2.0 0.8 slice_bitcast_fusion.7
  2.7 0.7 fusion
  3.5 0.7 slice_bitcast_fusion.5
  4.2 0.7 slice_bitcast_fusion.4
  4.9 0.6 pad.8.vtail_ref
  5.5 0.6 pad.7.ktail_ref
  6.1 0.7 copy.24
  6.8 0.7 and_reduce_fusion
  7.6 0.6 reshape.106.mask_ref
  8.1 176.7 %shard_map.128 = (bf16[128,4096]{1,0:T(8,128)(2,1)}, bf16[128,4096]{1,0:T(8,128)(2,1)}, bf16[4,1616,128]{2,1,0:T(8,128)(2,1)}, bf16[4,1616,128]{2,1,0:T(8,128)(2,1)}, f32[8,128]{1,0:T(8,128)}) custom-call(f32[1,1]{1,0:T(1,128)} %bitcast.gate_ref, f32[3,1,128]{2,1,0:T(1,128)} %reshape.106.mask_ref, bf16[16,512]{1,0:T(8,128)(2,1)} %pad.7.ktail_ref, ...), custom_call_target="tpu_custom_call" | custom-call | flops 30217863168 | bytes 11000000 | tf_op jit(solution)/shard_map/pallas_call | solution.py:504
  184.8 1.3 reduce_sum.9
  186.7 3.3 %slice_bitcast_fusion = (bf16[1601,4,128]{2,0,1:T(8,128)(2,1)}, bf16[1601,4,128]{2,0,1:T(8,128)(2,1)S(1)}) fusion(bf16[4,1616,128]{2,1,0:T(8,128)(2,1)} %get-tuple-element.13, bf16[4,1616,128]{2,1,0:T(8,128)(2,1)} %get-tuple-element.12), kind=kLoop, calls=%fused_computation | loop fusion | bytes 6557696 | tf_op jit(solution)/shard_map/transpose | solution.py:570
  190.1 2.7 %copy.19 = bf16[1601,4,128]{0,2,1:T(8,128)(2,1)S(1)} copy(bf16[1601,4,128]{2,0,1:T(8,128)(2,1)} %get-tuple-element.29) | data formatting | bytes 3278848 | tf_op jit(solution)/shard_map/transpose | solution.py:570
  192.8 2.3 %copy.21 = bf16[1,1,1601,512]{3,2,1,0:T(8,128)(2,1)} copy(bf16[1,1,1601,512]{2,3,1,0:T(8,128)(2,1)S(1)} %bitcast.32) | data formatting | bytes 3278848
  195.1 1.4 copy.18
  196.5 0.0 copy-start.1
  196.5 2.3 %copy.20 = bf16[1,1,1601,512]{3,2,1,0:T(8,128)(2,1)} copy(bf16[1,1,1601,512]{2,3,1,0:T(8,128)(2,1)S(1)} %bitcast.33) | data formatting | bytes 3278848
  198.8 0.0 copy-done.1
  198.8 0.0 copy-start
  198.8 1.0 copy.28
  199.7 0.6 copy-done
  200.4 1.0 copy.29
  (2 shorter events, 0.0 us)
Async XLA Ops:
  196.5 2.3 %copy-start.1 = (bf16[128,4096]{1,0:T(8,128)(2,1)S(1)}, bf16[128,4096]{1,0:T(8,128)(2,1)}, u32[]{:S(2)}) copy-start(bf16[128,4096]{1,0:T(8,128)(2,1)} %get-tuple-element.10) | copy-start | bytes 3145732
  198.8 1.6 copy-start

commit v2 on v1

--- a/solution.py
+++ b/solution.py
@@ -16,9 +16,10 @@
 KEYS_ROWS = 1616
 KEYS_WIDE = 1664
 WIDTH = GROUP * HD
-PARTS = 4
-ROWS = 2 * BLK
-CUTS = ((0, 512), (512, 512), (1024, 512), (1536, 80))
+HEADS = 4
+PARTS = GROUP // HEADS
+ROWS = HEADS * BLK
+CUTS = tuple((i * 256, min(256, KEYS_ROWS - i * 256)) for i in range(7))
 UNITS = 3 * KV
 LAG = 4
 SLOTS = LAG + 1
@@ -29,30 +30,53 @@
 F32 = jnp.float32
 BF16 = jnp.bfloat16
 MESH = pl.DeviceIdType.MESH
-NT = (((1,), (1,)), ((), ()))
 
 
 def mm(a, b):
     return jnp.dot(a, b, preferred_element_type=F32)
 
 
-def mm_nt(a, b):
-    return lax.dot_general(a, b, NT, preferred_element_type=F32)
-
-
-def stack_rows(pair):
-    return jnp.concatenate([pair[:, :HD], pair[:, HD:]], axis=0)
-
-
-def turn(pair):
-    return jnp.concatenate([pair[:, :HD].T, pair[:, HD:].T], axis=1)
+def pieces(wide):
+    return [wide[:, g * BLK : (g + 1) * BLK] for g in range(HEADS)]
+
+
+def stack_rows(chunk):
+    return jnp.concatenate(pieces(chunk), axis=0)
+
+
+def turn(chunk):
+    return jnp.concatenate([piece.T for piece in pieces(chunk)], axis=1)
+
+
+def slot_tables():
+    free, held, fwd, bwd = list(range(SLOTS)), {}, [], []
+    for step in range(UNITS + LAG):
+        if step < UNITS:
+            held[step // 3, (step + 2) % 3] = free.pop(0)
+            fwd.append(held[step // 3, (step + 2) % 3])
+        if step >= LAG:
+            old = step - LAG
+            bwd.append(held.pop((old // 3, old % 3)))
+            free.append(bwd[-1])
+    return fwd, bwd
+
+
+FWD_SLOT, BWD_SLOT = slot_tables()
+
+
+def pick(table, index):
+    found = jnp.int32(table[0])
+    for place, value in enumerate(table[1:], 1):
+        found = jnp.where(index == place, value, found)
+    return found
 
 
 def kernel(
     ring,
     rounds,
     gate_ref,
-    mask_ref,
+    list_ref,
+    range_ref,
     ktail_ref,
     vtail_ref,
     q_hbm,
@@ -64,6 +88,9 @@
     dk_hbm,
     dv_hbm,
     gsum_ref,
+    mask_ref,
+    rmax,
+    sbuf,
     qb,
     cb,
     kp,
@@ -83,6 +110,7 @@
     lse_out,
     lse_in,
     cvec,
+    dot,
     gacc,
     gsend,
     grecv,
@@ -200,7 +228,9 @@
     def store_kv(which, h):
         src, dst = ((kp, dk_hbm), (vp, dv_hbm))[which]
         return pltpu.make_async_copy(
-            src.at[h, pl.ds(0, KEYS_ROWS)], dst.at[h], s_kvout.at[which, h]
+            src.at[h, pl.ds(0, KEYS_ROWS)],
+            dst.at[:, pl.ds(pl.multiple_of(h * HD, HD), HD)],
+            s_kvout.at[which, h],
         )
 
     def store_att(h):
@@ -224,20 +254,29 @@
         pl.semaphore_signal(barrier, inc=1, device_id=gate_partner(r), device_id_type=MESH)
     pl.semaphore_wait(barrier, 2 + total_rounds)
 
-    for h in range(KV):
+    def send_inputs(h):
         for d in range(2):
             send_q(d, h).start()
         for d in range(2):
             send_c(d, h).start()
 
+    send_inputs(0)
     gacc[...] = jnp.zeros_like(gacc)
+    for p, (block, slot) in enumerate(((left, 1), (right, 1), (me, 0))):
+        tokens = pl.ds(pl.multiple_of(block * BLK, BLK), BLK)
+        first, last = range_ref[0:1, tokens], range_ref[1:2, tokens]
+        listed = jnp.where(list_ref[slot, block] == me, 1.0, 0.0).astype(F32)
+        mask_ref[p] = jnp.where((first <= slot) & (slot < last), 1.0, 0.0).astype(F32) * listed
 
     def prepare(h, _):
         for which in range(2):
             load_kv(which, h).wait()
         lanes = pl.ds(pl.multiple_of(h * HD, HD), HD)
         for tail, dst, flipped in ((ktail_ref, kp, kt), (vtail_ref, vp, vt)):
-            dst[h, KEYS_MAIN:KEYS_ROWS, :] = tail[:, lanes]
+            rows = lax.broadcasted_iota(jnp.int32, (KEYS_ROWS - KEYS_MAIN, HD), 0)
+            dst[h, KEYS_MAIN:KEYS_ROWS, :] = jnp.where(
+                rows < KEYS - KEYS_MAIN, tail[:, lanes].astype(F32), 0.0
+            ).astype(BF16)
             dst[h, KEYS_ROWS:, :] = jnp.zeros((KEYS_WIDE - KEYS_ROWS, HD), BF16)
             for j in range(KEYS_WIDE // HD):
                 piece = dst[h, j * HD : (j + 1) * HD, :]
@@ -245,6 +284,7 @@
         return 0
 
     lax.fori_loop(0, KV, prepare, 0)
+    send_inputs(1)
 
     def combine(h):
         send_stat(0, h).wait_recv()
@@ -276,69 +316,85 @@
         store_att(h).start()
         store_dq(h).start()
 
-    def forward_chunk(u, c):
-        h, p, slot = u // 3, u % 3, u % SLOTS
-        lanes = pl.ds(pl.multiple_of(c * ROWS, ROWS), ROWS)
-        query = stack_rows(qb[p, h, :, lanes])
-        row_max = None
-        for start, size in CUTS:
-            scores = mm_nt(kp[h, start : start + size, :], query)
-            if start + size > KEYS:
-                position = lax.broadcasted_iota(jnp.int32, scores.shape, 0)
-                scores = jnp.where(position < KEYS - start, scores, LOW)
-            pbuf[slot, c, start : start + size, :] = scores
-            part = jnp.max(scores, axis=0, keepdims=True)
-            row_max = part if row_max is None else jnp.maximum(row_max, part)
-        row_max = row_max * FACTOR
-        total = jnp.zeros((1, ROWS), F32)
-        out = jnp.zeros((HD, ROWS), F32)
-        for start, size in CUTS:
-            probs = jnp.exp2(pbuf[slot, c, start : start + size, :] * FACTOR - row_max)
-            pbuf[slot, c, start : start + size, :] = probs
-            total = total + jnp.sum(probs, axis=0, keepdims=True)
-            out = out + mm(vt[h, :, start : start + size], probs.astype(BF16))
-        onum[slot, c] = out
-        cot = turn(cb[p, h, :, lanes].astype(F32))
-        grad = (tanh * cot).astype(BF16).astype(F32)
-        delta = jnp.sum(grad * out, axis=0, keepdims=True) / total
-        gamma = jnp.sum(cot * out, axis=0, keepdims=True) / total
-        for kind, row in enumerate((row_max, total, delta, gamma)):
-            for g in range(2):
-                stats[slot, kind, pl.ds(2 * c + g, 1), :] = row[:, g * BLK : (g + 1) * BLK]
-
-    def backward_chunk(u, c):
-        h, p, slot = u // 3, u % 3, u % SLOTS
-        lanes = pl.ds(pl.multiple_of(c * ROWS, ROWS), ROWS)
-        query = stack_rows(qb[p, h, :, lanes])
-        grad = (tanh * stack_rows(cb[p, h, :, lanes]).astype(F32)).astype(BF16)
-        rows = [cvec[i, pl.ds(2 * c + g, 1), :] for i in range(2) for g in range(2)]
-        weight = jnp.concatenate(rows[:2], axis=1)
-        delta = jnp.concatenate(rows[2:], axis=1)
-        turned = jnp.zeros((HD, ROWS), F32)
+    def side_of(u):
+        return lax.rem(u + 2, 3)
+
+    def chunk_lanes(c):
+        return pl.ds(pl.multiple_of(c * ROWS, ROWS), ROWS)
+
+    def chunk(u, c, scoring, weighing, backing):
+        if scoring:
+            ahead = jnp.int32(0) if not weighing else jnp.minimum(u * PARTS + c + 1, UNITS * PARTS - 1)
+            ua, ca = ahead // PARTS, lax.rem(ahead, PARTS)
+            ha, pa = ua // 3, side_of(ua)
+            query_ahead = turn(qb[pa, ha, :, chunk_lanes(ca)])
+            next_max = None
+        if weighing:
+            h, p, slot = u // 3, side_of(u), pick(FWD_SLOT, u)
+            row_max = rmax[...] * FACTOR
+            total = jnp.zeros((1, ROWS), F32)
+            out = jnp.zeros((HD, ROWS), F32)
+        if backing:
+            ub = u - LAG
+            hb, pb, slotb = ub // 3, lax.rem(ub, 3), pick(BWD_SLOT, ub)
+            lanes = chunk_lanes(c)
+            query = stack_rows(qb[pb, hb, :, lanes])
+            grad = (tanh * stack_rows(cb[pb, hb, :, lanes]).astype(F32)).astype(BF16)
+            grad_t = dot[slotb, c]
+            rows = [cvec[i, pl.ds(HEADS * c + g, 1), :] for i in range(2) for g in range(HEADS)]
+            weight = jnp.concatenate(rows[:HEADS], axis=1)
+            delta = jnp.concatenate(rows[HEADS:], axis=1)
+            turned = jnp.zeros((HD, ROWS), F32)
         for start, size in CUTS:
             keys = slice(start, start + size)
-            probs = pbuf[slot, c, keys, :] * weight
-            prob_grad = mm_nt(vp[h, keys, :], grad)
-            score_grad = (probs * (prob_grad - delta)).astype(BF16)
-            dv_acc[keys, :] += mm(probs.astype(BF16), grad)
-            dk_acc[keys, :] += mm(score_grad, query)
-            turned = turned + mm(kt[h, :, keys], score_grad)
-        turned = turned * SCALE
-        out = onum[slot, c] * (weight * tanh)
-        dq = jnp.concatenate([turned[:, :BLK].T, turned[:, BLK:].T], axis=1).astype(BF16)
-        out = jnp.concatenate([out[:, :BLK].T, out[:, BLK:].T], axis=1)
-        qb[p, h, :, lanes] = dq
-
-        @pl.when(p < 2)
-        def _():
-            cb[p, h, :, lanes] = out.astype(BF16)
-
-        @pl.when(p == 2)
-        def _():
-            own_o[h, :, lanes] = out
+            if backing:
+                probs = pbuf[slotb, c, keys, :] * weight
+                prob_grad = mm(vp[hb, keys, :], grad_t)
+                score_grad = (probs * (prob_grad - delta)).astype(BF16)
+                dv_acc[keys, :] += mm(probs.astype(BF16), grad)
+                dk_acc[keys, :] += mm(score_grad, query)
+                turned = turned + mm(kt[hb, :, keys], score_grad)
+            if weighing:
+                fresh = jnp.exp2(sbuf[keys, :] * FACTOR - row_max)
+                pbuf[slot, c, keys, :] = fresh
+                total = total + jnp.sum(fresh, axis=0, keepdims=True)
+                out = out + mm(vt[h, :, keys], fresh.astype(BF16))
+            if scoring:
+                scores = mm(kp[ha, keys, :], query_ahead)
+                if start + size > KEYS:
+                    position = lax.broadcasted_iota(jnp.int32, scores.shape, 0)
+                    scores = jnp.where(position < KEYS - start, scores, LOW)
+                sbuf[keys, :] = scores
+                part = jnp.max(scores, axis=0, keepdims=True)
+                next_max = part if next_max is None else jnp.maximum(next_max, part)
+        if weighing:
+            onum[slot, c] = out
+            cot = turn(cb[p, h, :, chunk_lanes(c)].astype(F32))
+            fresh_grad = (tanh * cot).astype(BF16)
+            dot[slot, c] = fresh_grad
+            deltas = jnp.sum(fresh_grad.astype(F32) * out, axis=0, keepdims=True) / total
+            gammas = jnp.sum(cot * out, axis=0, keepdims=True) / total
+            for kind, row in enumerate((row_max, total, deltas, gammas)):
+                for g, piece in enumerate(pieces(row)):
+                    stats[slot, kind, pl.ds(HEADS * c + g, 1), :] = piece
+        if scoring:
+            rmax[...] = next_max
+        if backing:
+            turned = turned * SCALE
+            part = onum[slotb, c] * (weight * tanh)
+            part = turn(part)
+            qb[pb, hb, :, lanes] = turn(turned).astype(BF16)
+
+            @pl.when(pb < 2)
+            def _():
+                cb[pb, hb, :, lanes] = part.astype(BF16)
+
+            @pl.when(pb == 2)
+            def _():
+                own_o[hb, :, lanes] = part
 
     def forward_start(u):
-        h, p = u // 3, u % 3
+        h, p = u // 3, side_of(u)
 
         for d in range(2):
 
@@ -346,6 +402,12 @@
             def _():
                 send_q(d, h).wait_recv()
                 send_c(d, h).wait_recv()
+
+        for later in range(2, KV):
+
+            @pl.when(u == 3 * later - 5)
+            def _():
+                send_inputs(later)
 
         @pl.when(p == 2)
         def _():
@@ -353,7 +415,7 @@
             own_c(h).wait()
 
     def forward_end(u):
-        h, p, slot = u // 3, u % 3, u % SLOTS
+        h, p, slot = u // 3, side_of(u), pick(FWD_SLOT, u)
         on = mask_ref[p] > 0.0
         for kind, fill in enumerate((LOW, 0.0, 0.0, 0.0)):
             stats_out[p, h, kind] = jnp.where(on, stats[slot, kind], fill)
@@ -364,7 +426,7 @@
                 send_stat(d, h).start()
 
     def backward_start(u):
-        h, p, slot = u // 3, u % 3, u % SLOTS
+        h, p, slot = u // 3, u % 3, pick(BWD_SLOT, u)
         on = mask_ref[p] > 0.0
         for d in range(2):
 
@@ -400,35 +462,35 @@
             for which in range(2):
                 store_kv(which, h).start()
 
-    def events(u):
-        @pl.when((u >= 3) & (u <= UNITS) & (u % 3 == 0))
+    def chunk_events(u, c):
+        @pl.when((u >= 3) & (u <= UNITS) & (u % 3 == 0) & (c == PARTS // 2))
         def _():
             combine(u // 3 - 1)
 
-        @pl.when((u >= LAG + 3) & ((u - LAG) % 3 == 0))
+    def step_events(u):
+        @pl.when((u >= 9) & (u % 3 == 0))
         def _():
-            finalize((u - LAG) // 3 - 1)
-
-    def head_step(u, _):
-        forward_start(u)
-        events(u)
-        lax.fori_loop(0, PARTS, lambda c, x: (forward_chunk(u, c), x)[1], 0)
+            finalize(u // 3 - 3)
+
+    def step(u, backing):
+        step_events(u)
+        if backing:
+            backward_start(u - LAG)
+
+        def one(c, x):
+            chunk_events(u, c)
+
+            @pl.when((c == PARTS - 1) & (u < UNITS - 1))
+            def _():
+                forward_start(u + 1)
+
+            chunk(u, c, True, True, backing)
+            return x
+
+        lax.fori_loop(0, PARTS, one, 0)
         forward_end(u)
-        return 0
-
-    def main_step(u, _):
-        forward_start(u)
-        events(u)
-        backward_start(u - LAG)
-
-        def both(c, x):
-            forward_chunk(u, c)
-            backward_chunk(u - LAG, c)
-            return x
-
-        lax.fori_loop(0, PARTS, both, 0)
-        forward_end(u)
-        backward_end(u - LAG)
+        if backing:
+            backward_end(u - LAG)
         return 0
 
     def gate_round(r):
@@ -440,15 +502,16 @@
             send_gate(r).start()
 
     def tail_step(u, _):
-        events(u)
+        step_events(u)
         backward_start(u - LAG)
 
         def one(c, x):
-            backward_chunk(u - LAG, c)
+            chunk_events(u, c)
+            chunk(u, c, False, False, True)
             place = (u - UNITS) * PARTS + c
-            for r in range(total_rounds + 1):
-
-                @pl.when(place == 2 * r)
+            for r in range(total_rounds):
+
+                @pl.when(place == 1 + r)
                 def _():
                     gate_round(r)
 
@@ -458,11 +521,14 @@
         backward_end(u - LAG)
         return 0
 
-    lax.fori_loop(0, LAG, head_step, 0)
-    lax.fori_loop(LAG, UNITS, main_step, 0)
+    forward_start(jnp.int32(0))
+    chunk(0, 0, True, False, False)
+    lax.fori_loop(0, LAG, lambda u, x: step(u, False), 0)
+    lax.fori_loop(LAG, UNITS, lambda u, x: step(u, True), 0)
     lax.fori_loop(UNITS, UNITS + LAG, tail_step, 0)
+    gate_round(total_rounds)
     finalize(KV - 1)
-    gsum_ref[...] = gacc[...]
+    gsum_ref[0, 0] = (1.0 - tanh * tanh) * jnp.sum(gacc[...])
 
     for r in range(total_rounds):
         send_gate(r).wait_send()
@@ -479,40 +545,32 @@
         store_dq(h).wait()
 
 
-def tail_rows(tile):
-    return jnp.pad(tile[KEYS_MAIN:], ((0, KEYS_ROWS - KEYS), (0, 0)))
-
-
 def shards(ring, rounds, queries, image_keys, image_values, cotangent, gate, tile_list, slot_range):
-    position = lax.axis_index("seq")
     keys, values = image_keys[0, 0], image_values[0, 0]
     tanh = jnp.tanh(gate)
-    blocks = tile_list.shape[1]
-    ranges = slot_range[0].reshape(blocks, BLK, 2)
-    block = jnp.arange(blocks)[None, :]
-    side = position + jnp.array([-1, 1, 0])[:, None]
-    slot = jnp.array([1, 1, 0])[:, None]
-    listed = jnp.where(slot == 1, tile_list[0, :, 1][None], tile_list[0, :, 0][None])
-    chosen = (block == side) & (listed == position)
-    active = (ranges[None, :, :, 0] <= slot[..., None]) & (slot[..., None] < ranges[None, :, :, 1])
-    masks = jnp.any(chosen[..., None] & active, axis=1).astype(F32).reshape(3, 1, BLK)
-
     any_spec = pl.BlockSpec(memory_space=pl.ANY)
+    smem_spec = pl.BlockSpec(memory_space=pltpu.SMEM)
+    tail_rows = KEYS_ROWS - KEYS_MAIN
+    tail_spec = pl.BlockSpec((tail_rows, KV * HD), lambda i: (KEYS_MAIN // tail_rows, 0))
     vmem_spec = pl.BlockSpec(memory_space=pltpu.VMEM)
     sems = lambda *shape: pltpu.SemaphoreType.DMA(shape)
     total_rounds = rounds[0] + rounds[1]
-    attended, query_grad, key_out, value_out, gate_sum = pl.pallas_call(
+    attended, query_grad, key_out, value_out, gate_out = pl.pallas_call(
         functools.partial(kernel, ring, rounds),
         out_shape=(
             jax.ShapeDtypeStruct((BLK, KV * WIDTH), BF16),
             jax.ShapeDtypeStruct((BLK, KV * WIDTH), BF16),
-            jax.ShapeDtypeStruct((KV, KEYS_ROWS, HD), BF16),
-            jax.ShapeDtypeStruct((KV, KEYS_ROWS, HD), BF16),
-            jax.ShapeDtypeStruct((GROUP, BLK), F32),
+            jax.ShapeDtypeStruct((KEYS_ROWS, KV * HD), BF16),
+            jax.ShapeDtypeStruct((KEYS_ROWS, KV * HD), BF16),
+            jax.ShapeDtypeStruct((1, 1), F32),
         ),
-        in_specs=[pl.BlockSpec(memory_space=pltpu.SMEM)] + [vmem_spec] * 3 + [any_spec] * 4,
-        out_specs=(any_spec,) * 4 + (vmem_spec,),
+        grid=(1,),
+        in_specs=[smem_spec, smem_spec, vmem_spec, tail_spec, tail_spec] + [any_spec] * 4,
+        out_specs=(any_spec,) * 4 + (smem_spec,),
         scratch_shapes=[
+            pltpu.VMEM((3, 1, BLK), F32),
+            pltpu.VMEM((1, ROWS), F32),
+            pltpu.VMEM((KEYS_ROWS, ROWS), F32),
             pltpu.VMEM((3, KV, BLK, WIDTH), BF16),
             pltpu.VMEM((3, KV, BLK, WIDTH), BF16),
             pltpu.VMEM((KV, KEYS_WIDE, HD), BF16),
@@ -532,6 +590,7 @@
             pltpu.VMEM((KV, 2, GROUP, BLK), F32),
             pltpu.VMEM((2, KV, 2, GROUP, BLK), F32),
             pltpu.VMEM((2, GROUP, BLK), F32),
+            pltpu.VMEM((SLOTS, PARTS, HD, ROWS), BF16),
             pltpu.VMEM((GROUP, BLK), F32),
             pltpu.VMEM((total_rounds, GROUP, BLK), F32),
             pltpu.VMEM((total_rounds, GROUP, BLK), F32),
@@ -557,20 +616,23 @@
         ),
     )(
         tanh.reshape(1, 1),
-        masks,
-        tail_rows(keys),
-        tail_rows(values),
+        tile_list[0].T,
+        slot_range[0].T,
+        keys,
+        values,
         queries[0],
         cotangent[0],
         keys,
         values,
     )
 
-    def tile_of(grad):
-        return jnp.transpose(grad[:, :KEYS], (1, 0, 2)).reshape(1, 1, KEYS, KV * HD)
-
-    gate_grad = (1.0 - tanh * tanh) * jnp.sum(gate_sum)
-    return attended[None], query_grad[None], tile_of(key_out), tile_of(value_out), gate_grad
+    return (
+        attended[None],
+        query_grad[None],
+        key_out[None, None, :KEYS],
+        value_out[None, None, :KEYS],
+        gate_out.reshape(()),
+    )
 
 
 def solution(mesh):

time: 203 us -> 155 us (0.76)
  Pallas kernels: 177 us -> 144 us
  local copies, waits for them, and re-layouts: 19.2 us -> 6.51 us
  other arithmetic: 3.43 us -> 0 us
    pallas_call x1, Pallas kernels: 177 us -> 144 us  [shards(): pl.pallas_call(functools.partial(kernel, ring, rounds), out_shape=(jax.Sh...]
    transpose x3 -> x0, local copies, waits for them, and re-layouts: 7.47 us -> none  [tile_of(): return jnp.transpose(grad[:, :KEYS], (1, 0, 2)).reshape(1, 1, KEYS, KV * HD)]
    unnamed x9 -> x6, local copies, waits for them, and re-layouts: 7.81 us -> 2.57 us
    broadcast_in_dim x1, local copies, waits for them, and re-layouts: 0.76 us -> 3.94 us  [shards(): value_out[None, None, :KEYS]]
where the time goes in v2:
time: 155 us; the launch traced here: 154 us
  Pallas kernels  144 us (93%)
  local copies, waits for them, and re-layouts  6.51 us (4%)
  between operations  3.1 us (2%)
    pallas_call x1, Pallas kernels, shards(): pl.pallas_call(functools.partial(kernel, ring, rounds), out_shape=(jax.Sh...  144 us
    broadcast_in_dim x1, local copies, waits for them, and re-layouts, shards(): value_out[None, None, :KEYS]  3.94 us

profile of v2, /device:TPU:0, one launch (start us, length us, event | category | flops | bytes accessed | tf_op | source)
XLA Modules:
  0.0 153.5 jit_solution(12067688751230211062)
XLA Ops:
  1.3 143.9 %shard_map.110 = (bf16[128,4096]{1,0:T(8,128)(2,1)}, bf16[128,4096]{1,0:T(8,128)(2,1)}, bf16[1616,512]{1,0:T(8,128)(2,1)}, bf16[1616,512]{1,0:T(8,128)(2,1)}, f32[1,1]{1,0:T(1,128)}) custom-call(f32[1,1]{1,0:T(1,128)} %bitcast.gate_ref, s32[2,16]{1,0:T(2,128)} %bitcast.27, s32[2,2048]{1,0:T(2,128)} %bitcast.26, bf16[1601,512]{1,0:T(8,128)(2,1)} %bitcast.20, ...), custom_call_target="tpu_custom_call" | custom-call | flops 30217863168 | bytes 11000000 | tf_op jit(solution)/shard_map/pallas_call | solution.py:558
  145.2 0.0 copy-start.1
  145.2 3.9 %slice_bitcast_fusion = (bf16[1,1,1601,512]{3,2,1,0:T(8,128)(2,1)}, bf16[1,1,1601,512]{3,2,1,0:T(8,128)(2,1)}) fusion(bf16[1616,512]{1,0:T(8,128)(2,1)} %get-tuple-element.13, bf16[1616,512]{1,0:T(8,128)(2,1)} %get-tuple-element.12), kind=kLoop, calls=%fused_computation | loop fusion | bytes 6557696 | tf_op jit(solution)/shard_map/broadcast_in_dim | solution.py:633
  149.2 0.0 copy-start
  149.2 0.0 copy-done.1
  149.2 1.0 copy.16
  150.2 0.6 copy-done
  150.8 1.0 copy.17
Async XLA Ops:
  145.2 4.0 %copy-start.1 = (bf16[128,4096]{1,0:T(8,128)(2,1)S(1)}, bf16[128,4096]{1,0:T(8,128)(2,1)}, u32[]{:S(2)}) copy-start(bf16[128,4096]{1,0:T(8,128)(2,1)} %get-tuple-element.10) | copy-start | bytes 3145732
  149.2 1.6 %copy-start = (bf16[128,4096]{1,0:T(8,128)(2,1)S(1)}, bf16[128,4096]{1,0:T(8,128)(2,1)}, u32[]{:S(2)}) copy-start(bf16[128,4096]{1,0:T(8,128)(2,1)} %get-tuple-element.11) | copy-start | bytes 3145732

commit v3 on v2

--- a/solution.py
+++ b/solution.py
@@ -23,6 +23,8 @@
 UNITS = 3 * KV
 LAG = 4
 SLOTS = LAG + 1
+FWD_SIDE = (2, 0, 1) * KV
+BWD_SIDE = (2, 0, 1) * (KV - 1) + (0, 1, 2)
 LOW = -1e30
 SCALE = HD**-0.5
 LOG2E = 1.4426950408889634
@@ -52,11 +54,11 @@
     free, held, fwd, bwd = list(range(SLOTS)), {}, [], []
     for step in range(UNITS + LAG):
         if step < UNITS:
-            held[step // 3, (step + 2) % 3] = free.pop(0)
-            fwd.append(held[step // 3, (step + 2) % 3])
+            held[step // 3, FWD_SIDE[step]] = free.pop(0)
+            fwd.append(held[step // 3, FWD_SIDE[step]])
         if step >= LAG:
             old = step - LAG
-            bwd.append(held.pop((old // 3, old % 3)))
+            bwd.append(held.pop((old // 3, BWD_SIDE[old])))
             free.append(bwd[-1])
     return fwd, bwd
 
@@ -178,22 +180,25 @@
             device_id_type=MESH,
         )
 
-    def send_ro(p, h):
+    def chunk_lanes(c):
+        return pl.ds(pl.multiple_of(c * ROWS, ROWS), ROWS)
+
+    def send_ro(p, h, c):
         return pltpu.make_async_remote_copy(
-            src_ref=cb.at[p, h],
-            dst_ref=ret_o.at[1 - p, h],
-            send_sem=s_ro.at[0, p, h],
-            recv_sem=s_ro.at[1, 1 - p, h],
+            src_ref=cb.at[p, h, :, chunk_lanes(c)],
+            dst_ref=ret_o.at[1 - p, h, :, chunk_lanes(c)],
+            send_sem=s_ro.at[0, p, h, c],
+            recv_sem=s_ro.at[1, 1 - p, h, c],
             device_id={"seq": to_side(1 - p)},
             device_id_type=MESH,
         )
 
-    def send_rq(p, h):
+    def send_rq(p, h, c):
         return pltpu.make_async_remote_copy(
-            src_ref=qb.at[p, h],
-            dst_ref=ret_q.at[1 - p, h],
-            send_sem=s_rq.at[0, p, h],
-            recv_sem=s_rq.at[1, 1 - p, h],
+            src_ref=qb.at[p, h, :, chunk_lanes(c)],
+            dst_ref=ret_q.at[1 - p, h, :, chunk_lanes(c)],
+            send_sem=s_rq.at[0, p, h, c],
+            recv_sem=s_rq.at[1, 1 - p, h, c],
             device_id={"seq": to_side(1 - p)},
             device_id_type=MESH,
         )
@@ -284,7 +289,6 @@
         return 0
 
     lax.fori_loop(0, KV, prepare, 0)
-    send_inputs(1)
 
     def combine(h):
         send_stat(0, h).wait_recv()
@@ -307,8 +311,9 @@
 
     def finalize(h):
         for p in range(2):
-            send_ro(p, h).wait_recv()
-            send_rq(p, h).wait_recv()
+            for c in range(PARTS):
+                send_ro(p, h, c).wait_recv()
+                send_rq(p, h, c).wait_recv()
         cb[2, h] = (own_o[h] + ret_o[0, h].astype(F32) + ret_o[1, h].astype(F32)).astype(BF16)
         qb[2, h] = (
             qb[2, h].astype(F32) + ret_q[0, h].astype(F32) + ret_q[1, h].astype(F32)
@@ -319,8 +324,8 @@
     def side_of(u):
         return lax.rem(u + 2, 3)
 
-    def chunk_lanes(c):
-        return pl.ds(pl.multiple_of(c * ROWS, ROWS), ROWS)
+    def back_side(u):
+        return lax.rem(jnp.where(u < UNITS - 3, u + 2, u), 3)
 
     def chunk(u, c, scoring, weighing, backing):
         if scoring:
@@ -336,7 +341,7 @@
             out = jnp.zeros((HD, ROWS), F32)
         if backing:
             ub = u - LAG
-            hb, pb, slotb = ub // 3, lax.rem(ub, 3), pick(BWD_SLOT, ub)
+            hb, pb, slotb = ub // 3, back_side(ub), pick(BWD_SLOT, ub)
             lanes = chunk_lanes(c)
             query = stack_rows(qb[pb, hb, :, lanes])
             grad = (tanh * stack_rows(cb[pb, hb, :, lanes]).astype(F32)).astype(BF16)
@@ -385,34 +390,57 @@
             part = turn(part)
             qb[pb, hb, :, lanes] = turn(turned).astype(BF16)
 
-            @pl.when(pb < 2)
-            def _():
-                cb[pb, hb, :, lanes] = part.astype(BF16)
+            for d in range(2):
+
+                @pl.when(pb == d)
+                def _():
+                    cb[d, hb, :, lanes] = part.astype(BF16)
+                    send_ro(d, hb, c).start()
+                    send_rq(d, hb, c).start()
 
             @pl.when(pb == 2)
             def _():
                 own_o[hb, :, lanes] = part
 
-    def forward_start(u):
+    def wait_query(u):
         h, p = u // 3, side_of(u)
-
         for d in range(2):
 
             @pl.when(p == d)
             def _():
                 send_q(d, h).wait_recv()
+
+        @pl.when(p == 2)
+        def _():
+            own_q(h).wait()
+
+        @pl.when(u == 1)
+        def _():
+            for d in range(2):
+                send_q(d, 1).start()
+
+    def wait_cotangent(u):
+        h, p = u // 3, side_of(u)
+        for d in range(2):
+
+            @pl.when(p == d)
+            def _():
                 send_c(d, h).wait_recv()
 
-        for later in range(2, KV):
-
-            @pl.when(u == 3 * later - 5)
+        @pl.when(p == 2)
+        def _():
+            own_c(h).wait()
+
+        @pl.when(u == 1)
+        def _():
+            for d in range(2):
+                send_c(d, 1).start()
+
+        for later, place in ((2, 2), (3, 4)):
+
+            @pl.when(u == place)
             def _():
                 send_inputs(later)
-
-        @pl.when(p == 2)
-        def _():
-            own_q(h).wait()
-            own_c(h).wait()
 
     def forward_end(u):
         h, p, slot = u // 3, side_of(u), pick(FWD_SLOT, u)
@@ -426,7 +454,7 @@
                 send_stat(d, h).start()
 
     def backward_start(u):
-        h, p, slot = u // 3, u % 3, pick(BWD_SLOT, u)
+        h, p, slot = u // 3, back_side(u), pick(BWD_SLOT, u)
         on = mask_ref[p] > 0.0
         for d in range(2):
 
@@ -441,21 +469,15 @@
             cvec[0] = jnp.where(on, jnp.exp2(stats[slot, 0] - lse_out[h, 0]), 0.0)
             cvec[1] = lse_out[h, 1]
 
-        @pl.when(p == 0)
+        @pl.when(lax.rem(u, 3) == 0)
         def _():
             dk_acc[...] = jnp.zeros_like(dk_acc)
             dv_acc[...] = jnp.zeros_like(dv_acc)
 
     def backward_end(u):
-        h, p = u // 3, u % 3
-        for d in range(2):
-
-            @pl.when(p == d)
-            def _():
-                send_ro(d, h).start()
-                send_rq(d, h).start()
-
-        @pl.when(p == 2)
+        h = u // 3
+
+        @pl.when(lax.rem(u, 3) == 2)
         def _():
             kp[h, :KEYS_ROWS, :] = (dk_acc[...] * SCALE).astype(BF16)
             vp[h, :KEYS_ROWS, :] = dv_acc[...].astype(BF16)
@@ -474,6 +496,7 @@
 
     def step(u, backing):
         step_events(u)
+        wait_cotangent(u)
         if backing:
             backward_start(u - LAG)
 
@@ -482,7 +505,7 @@
 
             @pl.when((c == PARTS - 1) & (u < UNITS - 1))
             def _():
-                forward_start(u + 1)
+                wait_query(u + 1)
 
             chunk(u, c, True, True, backing)
             return x
@@ -521,7 +544,7 @@
         backward_end(u - LAG)
         return 0
 
-    forward_start(jnp.int32(0))
+    wait_query(jnp.int32(0))
     chunk(0, 0, True, False, False)
     lax.fori_loop(0, LAG, lambda u, x: step(u, False), 0)
     lax.fori_loop(LAG, UNITS, lambda u, x: step(u, True), 0)
@@ -538,8 +561,9 @@
             send_c(d, h).wait_send()
             send_stat(d, h).wait_send()
             send_lse(d, h).wait_send()
-            send_ro(d, h).wait_send()
-            send_rq(d, h).wait_send()
+            for c in range(PARTS):
+                send_ro(d, h, c).wait_send()
+                send_rq(d, h, c).wait_send()
             store_kv(d, h).wait()
         store_att(h).wait()
         store_dq(h).wait()
@@ -600,8 +624,8 @@
             sems(2, 2, KV),
             sems(2, 2, KV),
             sems(2, 2, KV),
-            sems(2, 2, KV),
-            sems(2, 2, KV),
+            sems(2, 2, KV, PARTS),
+            sems(2, 2, KV, PARTS),
             sems(2, KV),
             sems(2, KV),
             sems(2, total_rounds),

time: 155 us -> 144 us (0.929)
  the two profiles are of different devices: /device:TPU:0 before, /device:TPU:30 now
where the time goes in v3:
time: 144 us
  Pallas kernels  135 us (94%)
  local copies, waits for them, and re-layouts  6.51 us (5%)
  between operations  3.1 us (2%)
    pallas_call x1, Pallas kernels, shards(): pl.pallas_call(functools.partial(kernel, ring, rounds), out_shape=(jax.Sh...  135 us
    broadcast_in_dim x1, local copies, waits for them, and re-layouts, shards(): value_out[None, None, :KEYS]  3.94 us

profile of v3, /device:TPU:30, one launch (start us, length us, event | category | flops | bytes accessed | tf_op | source)
XLA Modules:
  0.0 144.2 jit_solution(11958852048417615013)
XLA Ops:
  1.3 134.6 %shard_map.110 = (bf16[128,4096]{1,0:T(8,128)(2,1)}, bf16[128,4096]{1,0:T(8,128)(2,1)}, bf16[1616,512]{1,0:T(8,128)(2,1)}, bf16[1616,512]{1,0:T(8,128)(2,1)}, f32[1,1]{1,0:T(1,128)}) custom-call(f32[1,1]{1,0:T(1,128)} %bitcast.gate_ref, s32[2,16]{1,0:T(2,128)} %bitcast.27, s32[2,2048]{1,0:T(2,128)} %bitcast.26, bf16[1601,512]{1,0:T(8,128)(2,1)} %bitcast.20, ...), custom_call_target="tpu_custom_call" | custom-call | flops 30217863168 | bytes 11000000 | tf_op jit(solution)/shard_map/pallas_call | solution.py:582
  136.0 0.0 copy-start.1
  136.0 3.9 %slice_bitcast_fusion = (bf16[1,1,1601,512]{3,2,1,0:T(8,128)(2,1)}, bf16[1,1,1601,512]{3,2,1,0:T(8,128)(2,1)}) fusion(bf16[1616,512]{1,0:T(8,128)(2,1)} %get-tuple-element.13, bf16[1616,512]{1,0:T(8,128)(2,1)} %get-tuple-element.12), kind=kLoop, calls=%fused_computation | loop fusion | bytes 6557696 | tf_op jit(solution)/shard_map/broadcast_in_dim | solution.py:657
  139.9 0.0 copy-start
  139.9 0.0 copy-done.1
  139.9 1.0 copy.16
  140.9 0.6 copy-done
  141.5 1.0 copy.17
Async XLA Ops:
  136.0 4.0 %copy-start.1 = (bf16[128,4096]{1,0:T(8,128)(2,1)S(1)}, bf16[128,4096]{1,0:T(8,128)(2,1)}, u32[]{:S(2)}) copy-start(bf16[128,4096]{1,0:T(8,128)(2,1)} %get-tuple-element.10) | copy-start | bytes 3145732
  139.9 1.6 %copy-start = (bf16[128,4096]{1,0:T(8,128)(2,1)S(1)}, bf16[128,4096]{1,0:T(8,128)(2,1)}, u32[]{:S(2)}) copy-start(bf16[128,4096]{1,0:T(8,128)(2,1)} %get-tuple-element.11) | copy-start | bytes 3145732

commit v4 on v3

--- a/solution.py
+++ b/solution.py
@@ -19,13 +19,14 @@
 HEADS = 4
 PARTS = GROUP // HEADS
 ROWS = HEADS * BLK
-CUTS = tuple((i * 256, min(256, KEYS_ROWS - i * 256)) for i in range(7))
+CUTS = ((0, 768), (768, 848))
 UNITS = 3 * KV
 LAG = 4
 SLOTS = LAG + 1
 FWD_SIDE = (2, 0, 1) * KV
 BWD_SIDE = (2, 0, 1) * (KV - 1) + (0, 1, 2)
 LOW = -1e30
+VMEM_LIMIT = 64 * 1024 * 1024 - 65536
 SCALE = HD**-0.5
 LOG2E = 1.4426950408889634
 FACTOR = SCALE * LOG2E
@@ -569,6 +570,12 @@
         store_dq(h).wait()
 
 
+def hand_on(*refs):
+    count = len(refs) // 2
+    for source, target in zip(refs[:count], refs[count:]):
+        target[...] = source[...]
+
+
 def shards(ring, rounds, queries, image_keys, image_values, cotangent, gate, tile_list, slot_range):
     keys, values = image_keys[0, 0], image_values[0, 0]
     tanh = jnp.tanh(gate)
@@ -631,7 +638,7 @@
             sems(2, total_rounds),
         ],
         compiler_params=pltpu.CompilerParams(
-            collective_id=0, has_side_effects=True, vmem_limit_bytes=64 * 1024 * 1024 - 65536
+            collective_id=0, has_side_effects=True, vmem_limit_bytes=VMEM_LIMIT
         ),
         cost_estimate=pl.CostEstimate(
             flops=2 * 6 * UNITS * 1024 * KEYS * HD,
@@ -650,11 +657,30 @@
         values,
     )
 
+    steps = 4
+    rows = BLK // steps
+    key_rows = -(-KEYS // (16 * steps)) * 16
+    token_spec = pl.BlockSpec((rows, KV * WIDTH), lambda i: (i, 0))
+    key_spec = pl.BlockSpec((key_rows, KV * HD), lambda i: (i, 0))
+    specs = (token_spec, token_spec, key_spec, key_spec)
+    attended, query_grad, key_grad, value_grad = pl.pallas_call(
+        hand_on,
+        out_shape=(
+            jax.ShapeDtypeStruct((BLK, KV * WIDTH), BF16),
+            jax.ShapeDtypeStruct((BLK, KV * WIDTH), BF16),
+            jax.ShapeDtypeStruct((KEYS, KV * HD), BF16),
+            jax.ShapeDtypeStruct((KEYS, KV * HD), BF16),
+        ),
+        grid=(steps,),
+        in_specs=specs,
+        out_specs=specs,
+        compiler_params=pltpu.CompilerParams(vmem_limit_bytes=VMEM_LIMIT),
+    )(attended, query_grad, key_out, value_out)
     return (
         attended[None],
         query_grad[None],
-        key_out[None, None, :KEYS],
-        value_out[None, None, :KEYS],
+        key_grad[None, None],
+        value_grad[None, None],
         gate_out.reshape(()),
     )
 

time: 144 us -> 138 us (0.958)
  the two profiles are of different devices: /device:TPU:30 before, /device:TPU:0 now
where the time goes in v4:
time: 138 us; the launch traced here: 136 us
  Pallas kernels  133 us (96%)
  between operations  3.09 us (2%)
    pallas_call x1, Pallas kernels, shards(): pl.pallas_call(functools.partial(kernel, ring, rounds), out_shape=(jax.Sh...  127 us
    pallas_call x1, Pallas kernels, shards(): pl.pallas_call(hand_on, out_shape=(jax.ShapeDtypeStruct((BLK, KV * WIDTH)...  5.35 us

profile of v4, /device:TPU:0, one launch (start us, length us, event | category | flops | bytes accessed | tf_op | source)
XLA Modules:
  0.0 135.9 jit_solution(1192771912058611476)
XLA Ops:
  1.3 127.5 %shard_map.110 = (bf16[128,4096]{1,0:T(8,128)(2,1)}, bf16[128,4096]{1,0:T(8,128)(2,1)}, bf16[1616,512]{1,0:T(8,128)(2,1)}, bf16[1616,512]{1,0:T(8,128)(2,1)}, f32[1,1]{1,0:T(1,128)}) custom-call(f32[1,1]{1,0:T(1,128)} %bitcast.gate_ref, s32[2,16]{1,0:T(2,128)} %bitcast.27, s32[2,2048]{1,0:T(2,128)} %bitcast.26, bf16[1601,512]{1,0:T(8,128)(2,1)} %bitcast.16, ...), custom_call_target="tpu_custom_call" | custom-call | flops 30217863168 | bytes 11000000 | tf_op jit(solution)/shard_map/pallas_call | solution.py:589
  128.8 5.4 %shard_map.111 = (bf16[128,4096]{1,0:T(8,128)(2,1)}, bf16[128,4096]{1,0:T(8,128)(2,1)}, bf16[1601,512]{1,0:T(8,128)(2,1)}, bf16[1601,512]{1,0:T(8,128)(2,1)}) custom-call(bf16[128,4096]{1,0:T(8,128)(2,1)} %get-tuple-element.14.refs_0_, bf16[128,4096]{1,0:T(8,128)(2,1)} %get-tuple-element.15.refs_1_, bf16[1616,512]{1,0:T(8,128)(2,1)} %get-tuple-element.16.refs_2_, ...), custom_call_target="tpu_custom_call" | custom-call | tf_op jit(solution)/shard_map/pallas_call | solution.py:666

commit v5 on v4

--- a/solution.py
+++ b/solution.py
@@ -415,11 +415,6 @@
         def _():
             own_q(h).wait()
 
-        @pl.when(u == 1)
-        def _():
-            for d in range(2):
-                send_q(d, 1).start()
-
     def wait_cotangent(u):
         h, p = u // 3, side_of(u)
         for d in range(2):
@@ -432,12 +427,7 @@
         def _():
             own_c(h).wait()
 
-        @pl.when(u == 1)
-        def _():
-            for d in range(2):
-                send_c(d, 1).start()
-
-        for later, place in ((2, 2), (3, 4)):
+        for later, place in ((1, 1), (2, 4), (3, 6)):
 
             @pl.when(u == place)
             def _():

time: 138 us -> 135 us (0.978)
  Pallas kernels: 133 us -> 129 us
    pallas_call x1, Pallas kernels: 127 us -> 124 us  [shards(): pl.pallas_call(functools.partial(kernel, ring, rounds), out_shape=(jax.Sh...]
where the time goes in v5:
time: 135 us; the launch traced here: 132 us
  Pallas kernels  129 us (96%)
  between operations  3.09 us (2%)
    pallas_call x1, Pallas kernels, shards(): pl.pallas_call(functools.partial(kernel, ring, rounds), out_shape=(jax.Sh...  124 us
    pallas_call x1, Pallas kernels, shards(): pl.pallas_call(hand_on, out_shape=(jax.ShapeDtypeStruct((BLK, KV * WIDTH)...  5.35 us

profile of v5, /device:TPU:0, one launch (start us, length us, event | category | flops | bytes accessed | tf_op | source)
XLA Modules:
  0.0 132.4 jit_solution(16854953536629514354)
XLA Ops:
  1.3 123.9 %shard_map.110 = (bf16[128,4096]{1,0:T(8,128)(2,1)}, bf16[128,4096]{1,0:T(8,128)(2,1)}, bf16[1616,512]{1,0:T(8,128)(2,1)}, bf16[1616,512]{1,0:T(8,128)(2,1)}, f32[1,1]{1,0:T(1,128)}) custom-call(f32[1,1]{1,0:T(1,128)} %bitcast.gate_ref, s32[2,16]{1,0:T(2,128)} %bitcast.27, s32[2,2048]{1,0:T(2,128)} %bitcast.26, bf16[1601,512]{1,0:T(8,128)(2,1)} %bitcast.16, ...), custom_call_target="tpu_custom_call" | custom-call | flops 30217863168 | bytes 11000000 | tf_op jit(solution)/shard_map/pallas_call | solution.py:579
  125.2 5.4 %shard_map.111 = (bf16[128,4096]{1,0:T(8,128)(2,1)}, bf16[128,4096]{1,0:T(8,128)(2,1)}, bf16[1601,512]{1,0:T(8,128)(2,1)}, bf16[1601,512]{1,0:T(8,128)(2,1)}) custom-call(bf16[128,4096]{1,0:T(8,128)(2,1)} %get-tuple-element.14.refs_0_, bf16[128,4096]{1,0:T(8,128)(2,1)} %get-tuple-element.15.refs_1_, bf16[1616,512]{1,0:T(8,128)(2,1)} %get-tuple-element.16.refs_2_, ...), custom_call_target="tpu_custom_call" | custom-call | tf_op jit(solution)/shard_map/pallas_call | solution.py:656

commit v6 on v5

--- a/solution.py
+++ b/solution.py
@@ -19,7 +19,7 @@
 HEADS = 4
 PARTS = GROUP // HEADS
 ROWS = HEADS * BLK
-CUTS = ((0, 768), (768, 848))
+CUTS = ((0, 1616),)
 UNITS = 3 * KV
 LAG = 4
 SLOTS = LAG + 1
@@ -93,7 +93,6 @@
     gsum_ref,
     mask_ref,
     rmax,
-    sbuf,
     qb,
     cb,
     kp,
@@ -260,13 +259,10 @@
         pl.semaphore_signal(barrier, inc=1, device_id=gate_partner(r), device_id_type=MESH)
     pl.semaphore_wait(barrier, 2 + total_rounds)
 
-    def send_inputs(h):
+    for send in (send_q, send_c):
         for d in range(2):
-            send_q(d, h).start()
-        for d in range(2):
-            send_c(d, h).start()
-
-    send_inputs(0)
+            send(d, 0).start()
+
     gacc[...] = jnp.zeros_like(gacc)
     for p, (block, slot) in enumerate(((left, 1), (right, 1), (me, 0))):
         tokens = pl.ds(pl.multiple_of(block * BLK, BLK), BLK)
@@ -333,11 +329,12 @@
             ahead = jnp.int32(0) if not weighing else jnp.minimum(u * PARTS + c + 1, UNITS * PARTS - 1)
             ua, ca = ahead // PARTS, lax.rem(ahead, PARTS)
             ha, pa = ua // 3, side_of(ua)
+            slota = pick(FWD_SLOT, ua)
             query_ahead = turn(qb[pa, ha, :, chunk_lanes(ca)])
             next_max = None
         if weighing:
             h, p, slot = u // 3, side_of(u), pick(FWD_SLOT, u)
-            row_max = rmax[...] * FACTOR
+            row_max = rmax[...]
             total = jnp.zeros((1, ROWS), F32)
             out = jnp.zeros((HD, ROWS), F32)
         if backing:
@@ -347,30 +344,32 @@
             query = stack_rows(qb[pb, hb, :, lanes])
             grad = (tanh * stack_rows(cb[pb, hb, :, lanes]).astype(F32)).astype(BF16)
             grad_t = dot[slotb, c]
-            rows = [cvec[i, pl.ds(HEADS * c + g, 1), :] for i in range(2) for g in range(HEADS)]
-            weight = jnp.concatenate(rows[:HEADS], axis=1)
-            delta = jnp.concatenate(rows[HEADS:], axis=1)
+            lse, delta, weight = (
+                jnp.concatenate(
+                    [cvec[i, pl.ds(HEADS * c + g, 1), :] for g in range(HEADS)], axis=1
+                )
+                for i in range(3)
+            )
             turned = jnp.zeros((HD, ROWS), F32)
         for start, size in CUTS:
             keys = slice(start, start + size)
             if backing:
-                probs = pbuf[slotb, c, keys, :] * weight
+                probs = jnp.exp2(pbuf[slotb, c, keys, :] - lse)
                 prob_grad = mm(vp[hb, keys, :], grad_t)
                 score_grad = (probs * (prob_grad - delta)).astype(BF16)
                 dv_acc[keys, :] += mm(probs.astype(BF16), grad)
                 dk_acc[keys, :] += mm(score_grad, query)
                 turned = turned + mm(kt[hb, :, keys], score_grad)
             if weighing:
-                fresh = jnp.exp2(sbuf[keys, :] * FACTOR - row_max)
-                pbuf[slot, c, keys, :] = fresh
+                fresh = jnp.exp2(pbuf[slot, c, keys, :] - row_max)
                 total = total + jnp.sum(fresh, axis=0, keepdims=True)
                 out = out + mm(vt[h, :, keys], fresh.astype(BF16))
             if scoring:
-                scores = mm(kp[ha, keys, :], query_ahead)
+                scores = mm(kp[ha, keys, :], query_ahead) * FACTOR
                 if start + size > KEYS:
                     position = lax.broadcasted_iota(jnp.int32, scores.shape, 0)
                     scores = jnp.where(position < KEYS - start, scores, LOW)
-                sbuf[keys, :] = scores
+                pbuf[slota, ca, keys, :] = scores
                 part = jnp.max(scores, axis=0, keepdims=True)
                 next_max = part if next_max is None else jnp.maximum(next_max, part)
         if weighing:
@@ -427,11 +426,18 @@
         def _():
             own_c(h).wait()
 
-        for later, place in ((1, 1), (2, 4), (3, 6)):
+        for later, place, sends in (
+            (1, 1, (send_q, send_c)),
+            (2, 4, (send_q, send_c)),
+            (3, 5, (send_q,)),
+            (3, 6, (send_c,)),
+        ):
 
             @pl.when(u == place)
             def _():
-                send_inputs(later)
+                for send in sends:
+                    for d in range(2):
+                        send(d, later).start()
 
     def forward_end(u):
         h, p, slot = u // 3, side_of(u), pick(FWD_SLOT, u)
@@ -446,19 +452,23 @@
 
     def backward_start(u):
         h, p, slot = u // 3, back_side(u), pick(BWD_SLOT, u)
-        on = mask_ref[p] > 0.0
+
+        def meet(lse, delta):
+            on = mask_ref[p] > 0.0
+            cvec[0] = jnp.where(on, lse, -LOW)
+            cvec[1] = delta
+            cvec[2] = jnp.where(on, jnp.exp2(stats[slot, 0] - lse), 0.0)
+
         for d in range(2):
 
             @pl.when(p == d)
             def _():
                 send_lse(d, h).wait_recv()
-                cvec[0] = jnp.where(on, jnp.exp2(stats[slot, 0] - lse_in[d, h, 0]), 0.0)
-                cvec[1] = lse_in[d, h, 1]
+                meet(lse_in[d, h, 0], lse_in[d, h, 1])
 
         @pl.when(p == 2)
         def _():
-            cvec[0] = jnp.where(on, jnp.exp2(stats[slot, 0] - lse_out[h, 0]), 0.0)
-            cvec[1] = lse_out[h, 1]
+            meet(lse_out[h, 0], lse_out[h, 1])
 
         @pl.when(lax.rem(u, 3) == 0)
         def _():
@@ -591,7 +601,6 @@
         scratch_shapes=[
             pltpu.VMEM((3, 1, BLK), F32),
             pltpu.VMEM((1, ROWS), F32),
-            pltpu.VMEM((KEYS_ROWS, ROWS), F32),
             pltpu.VMEM((3, KV, BLK, WIDTH), BF16),
             pltpu.VMEM((3, KV, BLK, WIDTH), BF16),
             pltpu.VMEM((KV, KEYS_WIDE, HD), BF16),
@@ -610,7 +619,7 @@
             pltpu.VMEM((2, KV, 4, GROUP, BLK), F32),
             pltpu.VMEM((KV, 2, GROUP, BLK), F32),
             pltpu.VMEM((2, KV, 2, GROUP, BLK), F32),
-            pltpu.VMEM((2, GROUP, BLK), F32),
+            pltpu.VMEM((3, GROUP, BLK), F32),
             pltpu.VMEM((SLOTS, PARTS, HD, ROWS), BF16),
             pltpu.VMEM((GROUP, BLK), F32),
             pltpu.VMEM((total_rounds, GROUP, BLK), F32),

time: 135 us -> 135 us (level)
  no operation moved by 1% of the time
where the time goes in v6:
time: 135 us; the launch traced here: 132 us
  Pallas kernels  129 us (96%)
  between operations  3.09 us (2%)
    pallas_call x1, Pallas kernels, shards(): pl.pallas_call(functools.partial(kernel, ring, rounds), out_shape=(jax.Sh...  124 us
    pallas_call x1, Pallas kernels, shards(): pl.pallas_call(hand_on, out_shape=(jax.ShapeDtypeStruct((BLK, KV * WIDTH)...  5.35 us

profile of v6, /device:TPU:0, one launch (start us, length us, event | category | flops | bytes accessed | tf_op | source)
XLA Modules:
  0.0 132.3 jit_solution(171904675184270515)
XLA Ops:
  1.3 123.8 %shard_map.110 = (bf16[128,4096]{1,0:T(8,128)(2,1)}, bf16[128,4096]{1,0:T(8,128)(2,1)}, bf16[1616,512]{1,0:T(8,128)(2,1)}, bf16[1616,512]{1,0:T(8,128)(2,1)}, f32[1,1]{1,0:T(1,128)}) custom-call(f32[1,1]{1,0:T(1,128)} %bitcast.gate_ref, s32[2,16]{1,0:T(2,128)} %bitcast.27, s32[2,2048]{1,0:T(2,128)} %bitcast.26, bf16[1601,512]{1,0:T(8,128)(2,1)} %bitcast.16, ...), custom_call_target="tpu_custom_call" | custom-call | flops 30217863168 | bytes 11000000 | tf_op jit(solution)/shard_map/pallas_call | solution.py:589
  125.2 5.4 %shard_map.111 = (bf16[128,4096]{1,0:T(8,128)(2,1)}, bf16[128,4096]{1,0:T(8,128)(2,1)}, bf16[1601,512]{1,0:T(8,128)(2,1)}, bf16[1601,512]{1,0:T(8,128)(2,1)}) custom-call(bf16[128,4096]{1,0:T(8,128)(2,1)} %get-tuple-element.14.refs_0_, bf16[128,4096]{1,0:T(8,128)(2,1)} %get-tuple-element.15.refs_1_, bf16[1616,512]{1,0:T(8,128)(2,1)} %get-tuple-element.16.refs_2_, ...), custom_call_target="tpu_custom_call" | custom-call | tf_op jit(solution)/shard_map/pallas_call | solution.py:665

commit v7 on v6

--- a/solution.py
+++ b/solution.py
@@ -19,7 +19,7 @@
 HEADS = 4
 PARTS = GROUP // HEADS
 ROWS = HEADS * BLK
-CUTS = ((0, 1616),)
+CUTS = ((0, 768), (768, 848))
 UNITS = 3 * KV
 LAG = 4
 SLOTS = LAG + 1

time: 135 us -> 137 us (1.015)
  Pallas kernels: 129 us -> 131 us
    pallas_call x1, Pallas kernels: 124 us -> 126 us  [shards(): pl.pallas_call(functools.partial(kernel, ring, rounds), out_shape=(jax.Sh...]
where the time goes in v7:
time: 137 us; the launch traced here: 135 us
  Pallas kernels  131 us (96%)
  between operations  3.09 us (2%)
    pallas_call x1, Pallas kernels, shards(): pl.pallas_call(functools.partial(kernel, ring, rounds), out_shape=(jax.Sh...  126 us
    pallas_call x1, Pallas kernels, shards(): pl.pallas_call(hand_on, out_shape=(jax.ShapeDtypeStruct((BLK, KV * WIDTH)...  5.35 us

profile of v7, /device:TPU:0, one launch (start us, length us, event | category | flops | bytes accessed | tf_op | source)
XLA Modules:
  0.0 134.5 jit_solution(7784621979942583427)
XLA Ops:
  1.3 126.1 %shard_map.110 = (bf16[128,4096]{1,0:T(8,128)(2,1)}, bf16[128,4096]{1,0:T(8,128)(2,1)}, bf16[1616,512]{1,0:T(8,128)(2,1)}, bf16[1616,512]{1,0:T(8,128)(2,1)}, f32[1,1]{1,0:T(1,128)}) custom-call(f32[1,1]{1,0:T(1,128)} %bitcast.gate_ref, s32[2,16]{1,0:T(2,128)} %bitcast.27, s32[2,2048]{1,0:T(2,128)} %bitcast.26, bf16[1601,512]{1,0:T(8,128)(2,1)} %bitcast.16, ...), custom_call_target="tpu_custom_call" | custom-call | flops 30217863168 | bytes 11000000 | tf_op jit(solution)/shard_map/pallas_call | solution.py:589
  127.4 5.4 %shard_map.111 = (bf16[128,4096]{1,0:T(8,128)(2,1)}, bf16[128,4096]{1,0:T(8,128)(2,1)}, bf16[1601,512]{1,0:T(8,128)(2,1)}, bf16[1601,512]{1,0:T(8,128)(2,1)}) custom-call(bf16[128,4096]{1,0:T(8,128)(2,1)} %get-tuple-element.14.refs_0_, bf16[128,4096]{1,0:T(8,128)(2,1)} %get-tuple-element.15.refs_1_, bf16[1616,512]{1,0:T(8,128)(2,1)} %get-tuple-element.16.refs_2_, ...), custom_call_target="tpu_custom_call" | custom-call | tf_op jit(solution)/shard_map/pallas_call | solution.py:665
